TPU v7x, 256 devices: a whole 4x4x8 slice. The times are simulated.
256 devices in a mesh: grp: 4 (over x), grid: 64 (over y, z, core).
Axes of the slice: x: 4, y: 4, z: 8, core: 2. Of those that a mesh axis runs over, the one named last changes fastest.
Arguments:
- orbitals: float32 [512, 262144], P('grp', 'grid'), may hold values from -6 to 6
- anchors: int32 [512, 3], replicated, may hold values from 0 to 31
- pair_slots: int32 [256, 4, 2], replicated, may hold values from -1 to 511, as said below
Outputs:
- exchange_term: float32 [512, 262144], P('grp', 'grid')
Inputs may be any that keep to these rules, and one draw needn't show every extreme that they name: `pair_slots`: row k lists the pairs of owner k, the device with index k in the order grp, grid; its first slots hold pairs of two different orbital numbers and its other slots hold -1 in both columns. Exactly 512 slots hold pairs in all, no row holds more than 4, and some row holds exactly 4.
All inputs are finite; a program needn't handle non-finite values.
Results may differ from a plain program's by a relative error of at most 0.0003.
Values sent between devices are 32-bit elements; how exact they have to be, the bound alone decides.
No kernel may reach another device: no remote copies, remote signals or barrier semaphores. Data moves between devices by JAX's collectives and lax.ppermute only.
A program may use at most 128 MiB of HBM per device.

v0:
```python
import functools

import jax
import jax.numpy as jnp
from jax import lax
from jax.experimental import pallas as pl
from jax.experimental.pallas import tpu as pltpu
from jax.sharding import PartitionSpec as P

B = 64
PAIR_DEV = 2
ITERS = 3
ROWS = B * B // 128
KEEP = 48
UNROLL = 16
TRIMMED = 56


def deal_evenly(pair_slots, owner_count, each_owner):
    flat_slots = pair_slots.reshape(-1, 2)
    filled = (flat_slots[:, 0] >= 0).astype(jnp.int32)
    order = jnp.arange(flat_slots.shape[0], dtype=jnp.int32)
    position = jnp.sum(jnp.where(order[None, :] < order[:, None], filled[None, :], 0), axis=1)
    wanted = lax.broadcasted_iota(jnp.int32, (owner_count, each_owner), 1) * owner_count
    wanted = (wanted + lax.broadcasted_iota(jnp.int32, (owner_count, each_owner), 0)).reshape(-1)
    matched = (position[None, :] == wanted[:, None]) & (filled[None, :] == 1)
    picked = jnp.dot(matched.astype(jnp.int32), flat_slots)
    return picked.reshape(owner_count, each_owner, 2)


def route_kernel(me_ref, pair_ref, anchor_ref, pos_ref, slot_ref, used_ref, mode_ref):
    me = me_ref[0]
    f32, i32 = jnp.float32, jnp.int32
    groups, each = 4, 2 * B

    def col(x):
        return jnp.sum(x, axis=1, keepdims=True)

    pairs = pair_ref[...].astype(f32).T
    at = lax.broadcasted_iota(i32, pairs.shape, 1)
    columns = [col(jnp.where(at == k, pairs, 0.0)) for k in range(pairs.shape[1])]
    a = jnp.concatenate(columns[0::2], axis=0).astype(i32)
    b = jnp.concatenate(columns[1::2], axis=0).astype(i32)
    n = a.shape[0]

    before = lax.broadcasted_iota(i32, (128, 128), 0) > lax.broadcasted_iota(i32, (128, 128), 1)
    before = jnp.where(before, 1.0, 0.0).astype(jnp.bfloat16)

    def sort_in(hot):
        width = hot.shape[1]
        totals = jnp.sum(hot, axis=0, keepdims=True)
        key = lax.broadcasted_iota(i32, (8, width), 1) & 15
        running = jnp.broadcast_to(totals, (8, width))
        for step in (1, 2, 4, 8):
            running = running + jnp.where(key >= step, pltpu.roll(running, step, axis=1), 0.0)
        below = running[0:1] - totals
        ranks, passed = [], below
        for k in range(0, n, 128):
            part = hot[k : k + 128]
            ahead = jnp.dot(before, part.astype(jnp.bfloat16), preferred_element_type=f32) + passed
            ranks.append(col(ahead * part))
            passed = passed + jnp.sum(part, axis=0, keepdims=True)
        return jnp.concatenate(ranks, axis=0), totals, below

    lane = lax.broadcasted_iota(i32, (n, 128), 1)
    valid = a >= 0
    ga, gb = a >> 7, b >> 7
    low, high = jnp.minimum(ga, gb), jnp.maximum(ga, gb)
    anchor_y = anchor_ref[1:2].astype(f32)
    name = lax.broadcasted_iota(i32, (n, anchor_ref.shape[1]), 1)
    oy = col(jnp.where(name == b, anchor_y, 0.0) - jnp.where(name == a, anchor_y, 0.0)).astype(i32)
    spare = jnp.abs(oy) >> 1
    kinds = lax.broadcasted_iota(i32, (n, 256), 1)
    hot = jnp.where(valid & (kinds == (low * groups + high) * 16 + spare), 1.0, 0.0)
    rank, sums, _ = sort_in(hot)
    sums = sums.astype(i32)
    kind1 = lax.broadcasted_iota(i32, (1, 256), 1) >> 4
    count, up = {}, {}
    for g in range(groups):
        for h in range(g, groups):
            count[g, h] = jnp.sum(jnp.where(kind1 == g * groups + h, sums, 0))
            up[g, h] = (count[g, h] >> 1) if h > g else 0

    def loads():
        load = [0] * groups
        for (g, h), c in count.items():
            load[g] = load[g] + (c - up[g, h])
            load[h] = load[h] + up[g, h]
        return load

    load = loads()
    for g, h in count:
        if h > g:
            up[g, h] = up[g, h] + ((load[g] - load[h] + 2) >> 2)
    load = loads()
    excess = 0
    for g in range(groups - 1):
        excess = excess + load[g] - each
        up[g, g + 1] = up[g, g + 1] + excess
    need = (ROWS * PAIR_DEV - TRIMMED) - 1
    fits = 1
    goes_up, there = jnp.zeros((1, 256), f32), jnp.ones((1, 256), f32)
    for (g, h), c in count.items():
        if h > g:
            u = up[g, h]
            fine = (u >= 0) & (u <= KEEP) & (c - u >= 0) & (c - u <= KEEP)
            fits = jnp.where(fine, fits, 0)
            goes_up = jnp.where(kind1 == g * groups + h, u.astype(f32), goes_up)
            there = jnp.where(kind1 == g * groups + h, jnp.maximum(c, 1).astype(f32), there)

    key1 = lax.broadcasted_iota(i32, (1, 256), 1) & 15
    weight = jnp.where(key1 <= need // 2, 1, 0) + jnp.where(key1 <= need // 2 + 1, 1, 0)
    small = {t: jnp.sum(jnp.where(kind1 == t[0] * groups + t[1], sums * weight, 0)).astype(f32) for t in count}
    share = goes_up / there
    surplus = jnp.zeros((1, 256), f32)
    for g in range(groups):
        held = jnp.zeros((1, 256), f32)
        for (low_g, high_g), amount in small.items():
            if low_g == high_g:
                held = held + (amount if low_g == g else 0.0)
            elif g in (low_g, high_g):
                part = jnp.sum(jnp.where((kind1 == low_g * groups + high_g) & (key1 == 0), share, 0.0))
                held = held + amount * (part if high_g == g else 1.0 - part)
        surplus = surplus + jnp.where((kind1 >> 2) == g, held, 0.0) - jnp.where((kind1 & 3) == g, held, 0.0)
    bend = surplus / (2.0 * jnp.maximum(goes_up, 1.0))
    most = jnp.minimum(there / jnp.maximum(goes_up, 1.0) - 1.0, 1.0)
    bend = jnp.clip(bend, -0.98 * most, 0.98 * most)
    u, c, bend = col(hot * goes_up), jnp.maximum(col(hot * there), 1.0), col(hot * bend)

    def risen_at(r):
        x = r / c
        return jnp.where(r >= c, u, jnp.clip(jnp.floor(u * (x + bend * x * (1.0 - x)) + 0.5 / c), 0.0, u))

    risen = risen_at(rank)
    rises = risen_at(rank + 1.0) > risen
    group = jnp.where(rises, high, low)
    source = low + high - group
    crosses = valid & (low != high)
    hot = jnp.where(valid & (lane == group * 16 + spare), 1.0, 0.0)
    order, keyed, below = sort_in(hot)
    order = order.astype(i32)
    second = order >= B
    q = jnp.where(second, B + each - 1 - order, order)
    lane1 = lax.broadcasted_iota(i32, (1, 128), 1)
    match = 1
    for g in range(groups):
        fits = jnp.where(jnp.sum(jnp.where((lane1 >> 4) == g, keyed, 0.0)) == each, fits, 0)
        for j in range(need // 2 + 1):
            both = (lane1 == g * 16 + j + 1) | (lane1 == g * 16 + need - j + 1)
            match = jnp.where(jnp.sum(jnp.where(both, below, 0.0)) <= each, match, 0)
    mode_ref[0] = jnp.where(fits == 1, 1 - match, 2)

    put = (((group - source) & 3) - 1) * KEEP + jnp.where(rises, risen, rank - risen).astype(i32)
    near_b = ga != group
    near = jnp.where(near_b, b, a) & 127
    far = jnp.where(near_b, a, b) & 127
    table = jnp.where(crosses, 128 + put, far)
    spare = spare * match
    moved = jnp.where(second, spare, 0)
    from_a = jnp.where(oy > 0, spare, 0) - moved
    from_b = jnp.where(oy < 0, spare, 0) - moved
    near_from, far_from = jnp.where(near_b, from_b, from_a), jnp.where(near_b, from_a, from_b)

    def side(*columns):
        at = lax.broadcasted_iota(i32, (n, 8), 1)
        out = jnp.zeros((n, 8), f32)
        for k, column in enumerate(columns):
            out = jnp.where(at == k, column.astype(f32), out)
        return out.astype(jnp.bfloat16)

    def spread(columns, mask):
        hot = jnp.where(mask, 1.0, 0.0).astype(jnp.bfloat16)
        out = lax.dot_general(columns, hot, (((0,), (0,)), ((), ())), preferred_element_type=f32)
        return out.astype(i32)

    mine = valid & (group == me)
    flag = jnp.where(near_b, 1, 0)
    columns = side(near, table & 255, a & 255, b & 255, flag, table >> 8, a >> 8, b >> 8)
    here = mine & (lane == q)
    got = spread(columns, here)
    more = spread(side(near_from + 16, far_from + 16, spare), here)
    pos_ref[...] = got
    pos_ref[1:4] = got[1:4] + 256 * got[5:8]
    pos_ref[6:7] = pos_ref[1:2]
    pos_ref[0:1] = got[0:1] * ROWS + more[0:1] - 16
    pos_ref[1:2] = pos_ref[6:7] * ROWS + more[1:2] - 16
    pos_ref[5:6] = more[2:3]
    wide = lax.broadcasted_iota(i32, (n, slot_ref.shape[1]), 1)
    here = wide == put
    zero = jnp.zeros_like(a)
    slots = spread(side(far, zero, zero + 1, far_from + 16), crosses & (source == me) & here)
    used_ref[...] = spread(side(q & (B - 1), q >> 6, spare), crosses & mine & here)
    slot_ref[...] = slots
    slot_ref[3:4] = slots[0:1] * ROWS + slots[3:4] - 16


def route(me, pair_slots, anchors):
    lists = jnp.transpose(pair_slots, (1, 2, 0)).reshape(-1, pair_slots.shape[0])
    width = 128 * -(-(3 * KEEP) // 128)
    vmem, smem = pl.BlockSpec(memory_space=pltpu.VMEM), pl.BlockSpec(memory_space=pltpu.SMEM)
    return pl.pallas_call(
        route_kernel,
        out_shape=[
            jax.ShapeDtypeStruct((8, 128), jnp.int32),
            jax.ShapeDtypeStruct((8, width), jnp.int32),
            jax.ShapeDtypeStruct((8, width), jnp.int32),
            jax.ShapeDtypeStruct((1,), jnp.int32),
        ],
        in_specs=[smem, vmem, vmem],
        out_specs=[vmem, vmem, vmem, smem],
        compiler_params=pltpu.CompilerParams(vmem_limit_bytes=40 << 20),
        cost_estimate=pl.CostEstimate(flops=10_000_000, bytes_accessed=1_000_000, transcendentals=0),
        name="route",
    )(me, lists, jnp.transpose(anchors))


def flat(ref):
    return ref.reshape(ref.shape[0] * ROWS, 128)


def fetch_kernel(row_of, idx_ref, table_ref, *refs):
    *outs, table, sem = refs
    copy = pltpu.make_async_copy(table_ref, table, sem)
    copy.start()
    copy.wait()
    for k, out_ref in enumerate(outs):
        count = out_ref.shape[0]

        def move(i, carry, out_ref=out_ref, k=k, count=count):
            out_ref[i] = row_of(idx_ref, table, k * count + i)
            return carry

        lax.fori_loop(0, count, move, 0, unroll=4)


def fetch(idx, table, row_of, name):
    return pl.pallas_call(
        functools.partial(fetch_kernel, row_of),
        out_shape=[jax.ShapeDtypeStruct((KEEP, ROWS, 128), jnp.float32)] * 3,
        in_specs=[pl.BlockSpec(memory_space=pltpu.SMEM), pl.BlockSpec(memory_space=pl.ANY)],
        out_specs=[pl.BlockSpec(memory_space=pltpu.VMEM)] * 3,
        scratch_shapes=[pltpu.VMEM(table.shape, jnp.float32), pltpu.SemaphoreType.DMA],
        compiler_params=pltpu.CompilerParams(vmem_limit_bytes=16 << 20),
        cost_estimate=pl.CostEstimate(flops=0, bytes_accessed=8_000_000, transcendentals=0),
        name=name,
    )(idx, table)


def sent_row(idx_ref, table, i):
    return table[idx_ref[0, i]]


def line_no():
    return lax.broadcasted_iota(jnp.int32, (ROWS, 128), 0)


def its_lines(s, spare, lines):
    keep = line_no() >= spare if s else line_no() < ROWS - spare
    return jnp.where(keep, lines, 0.0)


def deal_owner(pos_ref, row, p, table, out_ref, at):
    first, second = [table[pl.ds(pos_ref[row, s * B + p] + ROWS, ROWS)] for s in range(PAIR_DEV)]
    lines = out_ref.shape[1]
    cut = lines - ROWS
    out_ref[at, :cut] = first[:cut]
    if cut < ROWS:
        shared = lax.broadcasted_iota(jnp.int32, (ROWS - cut, 128), 0) + cut < ROWS - pos_ref[5, p]
        out_ref[at, cut:ROWS] = jnp.where(shared, first[cut:], second[: ROWS - cut])
    out_ref[at, ROWS:] = second[ROWS - cut :]


def clear_ends(table):
    zero = jnp.zeros((ROWS, 128), jnp.float32)
    table[0] = zero
    table[table.shape[0] - 1] = zero


PARTS = 4


def deal_near_kernel(pos_ref, orb_ref, near_ref, table, stage, near, sem_in, sem_out):
    pulls = [
        pltpu.make_async_copy(orb_ref.at[:, pl.ds(k * 1024, 1024)], stage.at[k], sem_in.at[k]) for k in range(PARTS)
    ]
    for copy in pulls:
        copy.start()
    clear_ends(table)
    for k, copy in enumerate(pulls):
        copy.wait()

        def lay_out(i, carry, k=k):
            rows = pl.ds(pl.multiple_of(i * 8, 8), 8)
            lines = [stage[k, rows, j * 128 : (j + 1) * 128] for j in range(8)]
            table[pl.ds(i * 8 + 1, 8), k * 8 : k * 8 + 8] = jnp.swapaxes(jnp.stack(lines), 0, 1)
            return carry

        lax.fori_loop(0, 128 // 8, lay_out, 0, unroll=2)
    pushes = []
    for k in range(PARTS):

        def owner(p, carry):
            deal_owner(pos_ref, 0, p, flat(table), near, p)
            return carry

        mine = pl.ds(k * (B // PARTS), B // PARTS)
        lax.fori_loop(k * (B // PARTS), (k + 1) * (B // PARTS), owner, 0, unroll=4)
        pushes.append(pltpu.make_async_copy(near.at[mine], near_ref.at[mine], sem_out.at[k]))
        pushes[-1].start()
    for copy in pushes:
        copy.wait()


def deal_near(lines, pos, orbitals):
    anywhere = pl.BlockSpec(memory_space=pl.ANY)
    dma = pltpu.SemaphoreType.DMA((PARTS,))
    return pl.pallas_call(
        deal_near_kernel,
        out_shape=jax.ShapeDtypeStruct((B, lines, 128), jnp.float32),
        in_specs=[pl.BlockSpec(memory_space=pltpu.SMEM), anywhere],
        out_specs=anywhere,
        scratch_shapes=[
            pltpu.VMEM((130, ROWS, 128), jnp.float32),
            pltpu.VMEM((PARTS, 128, 1024), jnp.float32),
            pltpu.VMEM((B, lines, 128), jnp.float32),
            dma,
            dma,
        ],
        compiler_params=pltpu.CompilerParams(vmem_limit_bytes=60 << 20),
        cost_estimate=pl.CostEstimate(flops=2_000_000, bytes_accessed=10_000_000, transcendentals=0),
        name="deal_near",
    )(pos, orbitals)


def deal_far_kernel(row, pos_ref, *refs):
    *parts, far_ref, table, sem = refs
    copies, end = [], 1
    for k, part in enumerate(parts):
        copies.append(pltpu.make_async_copy(part, table.at[pl.ds(end, part.shape[0])], sem.at[k]))
        end += part.shape[0]
    for copy in copies:
        copy.start()
    clear_ends(table)
    for copy in copies:
        copy.wait()

    def owner(p, carry):
        deal_owner(pos_ref, row, p, flat(table), far_ref, p)
        return carry

    lax.fori_loop(0, B, owner, 0, unroll=4)


def deal_far(lines, row, pos, parts):
    rows = sum(x.shape[0] for x in parts)
    return pl.pallas_call(
        functools.partial(deal_far_kernel, row),
        out_shape=jax.ShapeDtypeStruct((B, lines, 128), jnp.float32),
        in_specs=[pl.BlockSpec(memory_space=pltpu.SMEM)] + [pl.BlockSpec(memory_space=pl.ANY)] * len(parts),
        out_specs=pl.BlockSpec(memory_space=pltpu.VMEM),
        scratch_shapes=[pltpu.VMEM((rows + 2, ROWS, 128), jnp.float32), pltpu.SemaphoreType.DMA((len(parts),))],
        compiler_params=pltpu.CompilerParams(vmem_limit_bytes=63 << 20),
        cost_estimate=pl.CostEstimate(flops=0, bytes_accessed=12_000_000, transcendentals=0),
        name="deal_far",
    )(pos, *parts)


def solve_pair(offset, from_a, from_b, box_a, box_b, term_a, term_b, part, dens, resid, second, third, image):
    ox, oy, oz = offset
    shape = (ROWS, 128)
    line = lax.broadcasted_iota(jnp.int32, shape, 0)
    lane = lax.broadcasted_iota(jnp.int32, shape, 1)
    cy = 2 * line + (lane >> 6)
    cz = lane & (B - 1)
    high = lane >= B
    ends = (high & (line == 0)) | (~high & (line == ROWS - 1))
    no_up, no_down = cz == B - 1, cz == 0

    def plane(ref, x):
        return ref[pl.ds(pl.multiple_of(x * ROWS, ROWS), ROWS)]

    def put(ref, x, value):
        ref[pl.ds(pl.multiple_of(x * ROWS, ROWS), ROWS)] = value

    def shifter(sy, sz):
        flat = sy * B + sz
        lines, steps = flat >> 7, flat & 127
        inside = (cy >= sy) & (cy < B + sy) & (cz >= sz) & (cz < B + sz)
        keep = lane < 128 - steps

        def shift(ref, x, first):
            at = x * ROWS - lines - first
            moved = jnp.where(keep, ref[pl.ds(at, ROWS)], ref[pl.ds(at - 1, ROWS)])
            return jnp.where(inside, pltpu.roll(moved, steps, axis=1), 0.0)

        return shift

    def apply(ref, x):
        here = plane(ref, x + 1)
        at = (x + 1) * ROWS
        other = jnp.where(high, ref[pl.ds(at - 1, ROWS)], ref[pl.ds(at + 1, ROWS)])
        other = here + jnp.where(ends, 0.0, other)
        beside = plane(ref, x) + plane(ref, x + 2) + pltpu.roll(other, B, axis=1)
        upper = jnp.where(no_up, 0.0, pltpu.roll(here, 127, axis=1))
        lower = jnp.where(no_down, 0.0, pltpu.roll(here, 1, axis=1))
        return here, 6.0 * here - beside - upper - lower

    zero = jnp.zeros(shape, jnp.float32)
    for ref in (dens, second, third):
        put(ref, 0, zero)
        put(ref, B + 1, zero)

    shift_on = shifter(oy, oz)
    shift_back = shifter(-oy, -oz)

    def begin(x, acc):
        src = x - ox
        inside = jnp.where((src >= 0) & (src < B), 1.0, 0.0)
        moved = shift_on(box_b, jnp.clip(src, 0, B - 1) + 1, from_b) * inside
        density = box_a[pl.ds((x + 1) * ROWS - from_a, ROWS)] * moved
        put(part, x, moved)
        put(dens, x + 1, density)
        return acc + density * density

    def first(x, acc):
        here, img = apply(dens, x)
        put(image, x + 1, img)
        return acc + here * img

    norm0 = yield begin
    step0 = norm0 / (yield first)

    def rest0(x, acc):
        left = plane(dens, x + 1) - step0 * plane(image, x + 1)
        put(resid, x, left)
        return acc + left * left

    norm1 = yield rest0
    ratio0 = norm1 / norm0

    def turn1(x, acc):
        put(second, x + 1, plane(resid, x) + ratio0 * plane(dens, x + 1))
        return acc

    def again(x, acc):
        here, img = apply(second, x)
        put(image, x + 1, img)
        return acc + here * img

    yield turn1
    step1 = norm1 / (yield again)

    def rest1(x, acc):
        left = plane(resid, x) - step1 * plane(image, x + 1)
        put(resid, x, left)
        return acc + left * left

    norm2 = yield rest1
    ratio1 = norm2 / norm1

    def turn2(x, acc):
        put(third, x + 1, plane(resid, x) + ratio1 * plane(second, x + 1))
        return acc

    def last(x, acc):
        here, img = apply(third, x)
        return acc + here * img

    yield turn2
    step2 = norm2 / (yield last)

    def finish(x, acc):
        potential = step0 * plane(dens, x + 1) + step1 * plane(second, x + 1) + step2 * plane(third, x + 1)
        here = pl.ds((x + 1) * ROWS - from_a, ROWS)
        term_a[here] = potential * plane(part, x)
        put(image, x + 1, potential * box_a[here])
        return acc

    def back(x, acc):
        src = x + ox
        inside = jnp.where((src >= 0) & (src < B), 1.0, 0.0)
        term_b[pl.ds((x + 1) * ROWS - from_b, ROWS)] = shift_back(image, jnp.clip(src, 0, B - 1) + 1, 0) * inside
        return acc

    yield finish
    yield back


def run_together(solvers, unroll):
    steps = [next(solver) for solver in solvers]
    zero = jnp.zeros((ROWS, 128), jnp.float32)
    while True:
        def both(x, accs, steps=tuple(steps)):
            return tuple(step(x, acc) for step, acc in zip(steps, accs))

        accs = lax.fori_loop(0, B, both, (zero,) * len(steps), unroll=unroll)
        sums = [jnp.sum(acc, keepdims=True) for acc in accs]
        try:
            steps = [solver.send(value) for solver, value in zip(solvers, sums)]
        except StopIteration:
            return


def pair_kernel(place_ref, pos_ref, anchor_ref, near_ref, far_ref, near_out, far_out, boxes, terms, *rest):
    *fields, sem = rest
    lines = near_ref.shape[1]
    cut = lines - ROWS
    at = [s * B + place_ref[0] for s in range(PAIR_DEV)]
    flags = [pos_ref[4, k] for k in at]
    copies = []
    for s in range(PAIR_DEV):
        for k, ref in enumerate((near_ref, far_ref)):
            which = 1 - flags[s] if k else flags[s]
            source = ref.at[:, pl.ds(s * cut, ROWS)]
            copies.append(pltpu.make_async_copy(source, boxes.at[s, which, pl.ds(1, B)], sem.at[s, k]))
    for copy in copies:
        copy.start()
    for s in range(PAIR_DEV):
        for k in range(2):
            clear_ends(boxes.at[s, k])
    for copy in copies:
        copy.wait()
    solvers = []
    for s in range(PAIR_DEV):
        orb_a, orb_b = pos_ref[2, at[s]], pos_ref[3, at[s]]
        offset = [anchor_ref[3 * orb_b + k] - anchor_ref[3 * orb_a + k] for k in range(3)]
        spare = pos_ref[5, at[s]]
        moved = spare if s else 0
        from_a = jnp.where(offset[1] > 0, spare, 0) - moved
        from_b = jnp.where(offset[1] < 0, spare, 0) - moved
        refs = [flat(ref.at[s, k]) for ref in (boxes, terms) for k in range(2)]
        solvers.append(solve_pair(offset, from_a, from_b, *refs, *[ref.at[s] for ref in fields]))
    run_together(solvers, UNROLL if cut < ROWS else 1)

    def together(x, carry):
        for k, out in enumerate((near_out, far_out)):
            first, second = [terms[s, 1 - flags[s] if k else flags[s], x + 1] for s in range(PAIR_DEV)]
            out[x, :cut] = first[:cut]
            if cut < ROWS:
                low = its_lines(0, pos_ref[5, at[0]], first)[cut:]
                out[x, cut:ROWS] = low + its_lines(1, pos_ref[5, at[1]], second)[: ROWS - cut]
            out[x, ROWS:] = second[ROWS - cut :]
        return carry

    lax.fori_loop(0, B, together, 0, unroll=4)


def solve(place, pos, anchors, near, far):
    smem, vmem = pl.BlockSpec(memory_space=pltpu.SMEM), pl.BlockSpec(memory_space=pltpu.VMEM)
    anywhere = pl.BlockSpec(memory_space=pl.ANY)
    field = pltpu.VMEM((PAIR_DEV, B * ROWS, 128), jnp.float32)
    padded = pltpu.VMEM((PAIR_DEV, (B + 2) * ROWS, 128), jnp.float32)
    boxes = pltpu.VMEM((PAIR_DEV, 2, B + 2, ROWS, 128), jnp.float32)
    return pl.pallas_call(
        pair_kernel,
        out_shape=[jax.ShapeDtypeStruct(near.shape, jnp.float32)] * 2,
        in_specs=[smem, smem, smem, anywhere, anywhere],
        out_specs=[vmem, vmem],
        scratch_shapes=[
            boxes, boxes, field, padded, field, padded, padded, padded,
            pltpu.SemaphoreType.DMA((PAIR_DEV, 2)),
        ],
        compiler_params=pltpu.CompilerParams(vmem_limit_bytes=40 << 20),
        cost_estimate=pl.CostEstimate(flops=100_000_000, bytes_accessed=30_000_000, transcendentals=0),
        name="solve",
    )(place, pos, anchors, near, far)


def add_lines(total, line, lines):
    here = pl.ds(line + ROWS, ROWS)
    total[here] = total[here] + lines


def add_far_kernel(pos_ref, terms_ref, out_ref):
    out_ref[...] = jnp.zeros(out_ref.shape, jnp.float32)
    total = flat(out_ref)
    cut = terms_ref.shape[1] - ROWS

    def here(p, carry):
        for s in range(PAIR_DEV):
            q = s * B + p

            @pl.when(pos_ref[6, q] < 128)
            def _(q=q, s=s):
                lines = terms_ref[p, s * cut : s * cut + ROWS]
                add_lines(total, pos_ref[1, q], its_lines(s, pos_ref[5, q], lines))

        return carry

    lax.fori_loop(0, B, here, 0)


def add_far(pos, terms):
    smem, vmem = pl.BlockSpec(memory_space=pltpu.SMEM), pl.BlockSpec(memory_space=pltpu.VMEM)
    return pl.pallas_call(
        add_far_kernel,
        out_shape=jax.ShapeDtypeStruct((130, ROWS, 128), jnp.float32),
        in_specs=[smem, vmem],
        out_specs=vmem,
        compiler_params=pltpu.CompilerParams(vmem_limit_bytes=24 << 20),
        cost_estimate=pl.CostEstimate(flops=2_000_000, bytes_accessed=4_000_000, transcendentals=0),
        name="add_far",
    )(pos, terms)


def add_arrived_kernel(slot_ref, sum_ref, *refs):
    *from_groups, out_ref, sem = refs
    copy = pltpu.make_async_copy(sum_ref, out_ref, sem)
    copy.start()
    copy.wait()
    total = flat(out_ref)

    def there(k, carry):
        for d, ref in enumerate(from_groups):
            at = d * KEEP + k

            @pl.when(slot_ref[2, at] == 1)
            def _(at=at, ref=ref):
                add_lines(total, slot_ref[3, at], ref[k])

        return carry

    lax.fori_loop(0, KEEP, there, 0)


def add_arrived(slot, summed, from_groups):
    smem, vmem = pl.BlockSpec(memory_space=pltpu.SMEM), pl.BlockSpec(memory_space=pltpu.VMEM)
    return pl.pallas_call(
        add_arrived_kernel,
        out_shape=jax.ShapeDtypeStruct(summed.shape, jnp.float32),
        in_specs=[smem, pl.BlockSpec(memory_space=pl.ANY)] + [vmem] * 3,
        out_specs=vmem,
        scratch_shapes=[pltpu.SemaphoreType.DMA],
        compiler_params=pltpu.CompilerParams(vmem_limit_bytes=63 << 20),
        cost_estimate=pl.CostEstimate(flops=2_000_000, bytes_accessed=6_000_000, transcendentals=0),
        name="add_arrived",
    )(slot, summed, *from_groups)


def add_near_kernel(pos_ref, sum_ref, terms_ref, out_ref, acc, terms, stage, sem_sum, sem_in, sem_out):
    cut = terms.shape[1] - ROWS
    copies = [pltpu.make_async_copy(sum_ref, acc, sem_sum)]
    for k in range(PARTS):
        mine = pl.ds(k * (B // PARTS), B // PARTS)
        copies.append(pltpu.make_async_copy(terms_ref.at[mine], terms.at[mine], sem_in.at[k]))
    for copy in copies:
        copy.start()
    copies[0].wait()
    for k in range(PARTS):
        copies[k + 1].wait()

        def here(p, carry):
            for s in range(PAIR_DEV):
                q = s * B + p
                lines = terms[p, s * cut : s * cut + ROWS]
                add_lines(flat(acc), pos_ref[0, q], its_lines(s, pos_ref[5, q], lines))
            return carry

        lax.fori_loop(k * (B // PARTS), (k + 1) * (B // PARTS), here, 0, unroll=2)
    pushes = []
    for k in range(PARTS):

        def lay_out(i, carry, k=k):
            rows = pl.ds(pl.multiple_of(i * 8, 8), 8)
            lines = jnp.swapaxes(acc[pl.ds(i * 8 + 1, 8), k * 8 : k * 8 + 8], 0, 1)
            for j in range(8):
                stage[k, rows, j * 128 : (j + 1) * 128] = lines[j]
            return carry

        lax.fori_loop(0, 128 // 8, lay_out, 0, unroll=2)
        pushes.append(pltpu.make_async_copy(stage.at[k], out_ref.at[:, pl.ds(k * 1024, 1024)], sem_out.at[k]))
        pushes[-1].start()
    for copy in pushes:
        copy.wait()


def add_near(pos, summed, terms):
    anywhere = pl.BlockSpec(memory_space=pl.ANY)
    dma = pltpu.SemaphoreType.DMA((PARTS,))
    return pl.pallas_call(
        add_near_kernel,
        out_shape=jax.ShapeDtypeStruct((128, ROWS * 128), jnp.float32),
        in_specs=[pl.BlockSpec(memory_space=pltpu.SMEM), anywhere, anywhere],
        out_specs=anywhere,
        scratch_shapes=[
            pltpu.VMEM((130, ROWS, 128), jnp.float32),
            pltpu.VMEM(terms.shape, jnp.float32),
            pltpu.VMEM((PARTS, 128, 1024), jnp.float32),
            pltpu.SemaphoreType.DMA,
            dma,
            dma,
        ],
        compiler_params=pltpu.CompilerParams(vmem_limit_bytes=63 << 20),
        cost_estimate=pl.CostEstimate(flops=2_000_000, bytes_accessed=10_000_000, transcendentals=0),
        name="add_near",
    )(pos, summed, terms)


def turned(x, shift):
    groups = lax.axis_size("grp")
    return lax.ppermute(x, "grp", [(g, (g + shift) % groups) for g in range(groups)])


def exchanged(planes):
    return lax.all_to_all(planes, "grid", 0, 0, tiled=True)


def there_and_back(place, pos, anchors, both):
    lines = both.shape[1] // 2

    def solve_both(both):
        return jnp.concatenate(solve(place, pos, anchors, both[:, :lines], both[:, lines:]), axis=1)

    def step(k, both):
        return lax.cond(k == 0, solve_both, lambda x: x, exchanged(both))

    return lax.fori_loop(0, 2, step, both)


def fitting(lines, orbitals, anchors, place, pos, slot, used):
    def used_row(used_ref, table, i):
        p, s, spare = used_ref[0, i], used_ref[1, i], used_ref[2, i]
        plane = table[p, pl.ds(pl.multiple_of(s * (lines - ROWS), 8), ROWS)]
        keep = (line_no() >= s * spare) & (line_no() < ROWS - (1 - s) * spare)
        return jnp.where(keep, plane, 0.0)

    trimmed = lines == TRIMMED
    near = deal_near(lines, pos, orbitals)
    if trimmed:
        near = exchanged(near)
    local = orbitals.reshape(128, ROWS, 128)
    arrived = [turned(x, d) for d, x in enumerate(fetch(slot, local, sent_row, "send"), 1)]
    far = deal_far(lines, 1, pos, [local] + arrived)
    if trimmed:
        near_terms, far_terms = solve(place, pos, anchors.reshape(-1), near, exchanged(far))
        far_terms = exchanged(far_terms)
    else:
        both = there_and_back(place, pos, anchors.reshape(-1), jnp.concatenate([near, far], axis=1))
        near_terms, far_terms = both[:, :lines], both[:, lines:]
    from_groups = [turned(x, -d) for d, x in enumerate(fetch(used, far_terms, used_row, "back"), 1)]
    summed = add_far(pos, far_terms)
    if trimmed:
        near_terms = exchanged(near_terms)
    return add_near(pos, add_arrived(slot, summed, from_groups), near_terms)


def add_all_kernel(pos_ref, terms_ref, out_ref):
    out_ref[...] = jnp.zeros(out_ref.shape, jnp.float32)
    total = flat(out_ref)

    def here(p, carry):
        for s in range(PAIR_DEV):
            for k in range(2):
                at = (k * PAIR_DEV + s) * ROWS
                add_lines(total, pos_ref[k, s * B + p], terms_ref[p, at : at + ROWS])
        return carry

    lax.fori_loop(0, B, here, 0)


def add_all(pos, terms, count):
    return pl.pallas_call(
        add_all_kernel,
        out_shape=jax.ShapeDtypeStruct((count + 2, ROWS, 128), jnp.float32),
        in_specs=[pl.BlockSpec(memory_space=pltpu.SMEM), pl.BlockSpec(memory_space=pltpu.VMEM)],
        out_specs=pl.BlockSpec(memory_space=pltpu.VMEM),
        compiler_params=pltpu.CompilerParams(vmem_limit_bytes=32 << 20),
        cost_estimate=pl.CostEstimate(flops=2_000_000, bytes_accessed=10_000_000, transcendentals=0),
        name="add_all",
    )(pos, terms)


def general(orbitals, anchors, pair_slots, place):
    groups, grid_count = lax.axis_size("grp"), lax.axis_size("grid")
    me, rows = lax.axis_index("grp"), orbitals.shape[0]
    dealt = deal_evenly(pair_slots, groups * grid_count, PAIR_DEV)
    own = lax.dynamic_slice_in_dim(dealt, me * grid_count, grid_count, 0)
    own = jnp.maximum(jnp.transpose(own, (2, 1, 0)).reshape(2, PAIR_DEV * grid_count), 0)
    pos = jnp.concatenate([own * ROWS, own, jnp.zeros((4, own.shape[1]), jnp.int32)])
    round_trip = [turned(orbitals, d) for d in (3, 2, 1)] + [orbitals]
    pieces = lax.dynamic_slice_in_dim(jnp.concatenate(round_trip * 2), (3 - me) * rows, groups * rows, 0)
    table = pieces.reshape(-1, ROWS, 128)
    both = jnp.concatenate([deal_far(PAIR_DEV * ROWS, k, pos, [table]) for k in range(2)], axis=1)

    terms = there_and_back(place, pos, anchors.reshape(-1), both)
    summed = add_all(pos, terms, table.shape[0])
    blocks = [lax.dynamic_slice_in_dim(summed, ((me + d) & 3) * rows + 1, rows, 0) for d in range(4)]
    return (blocks[0] + sum(turned(blocks[d], d) for d in (1, 2, 3))).reshape(orbitals.shape)


def body(orbitals, anchors, pair_slots):
    me = lax.axis_index("grp").astype(jnp.int32)[None]
    place = lax.axis_index("grid").astype(jnp.int32)[None]
    pos, slot, used, mode = route(me, pair_slots, anchors)

    def other():
        return lax.cond(
            mode[0] == 1,
            lambda: fitting(PAIR_DEV * ROWS, orbitals, anchors, place, pos, slot, used),
            lambda: general(orbitals, anchors, pair_slots, place),
        )

    return lax.cond(mode[0] == 0, lambda: fitting(TRIMMED, orbitals, anchors, place, pos, slot, used), other)


def solution(mesh):
    return jax.shard_map(
        body,
        mesh=mesh,
        in_specs=(P("grp", "grid"), P(), P()),
        out_specs=P("grp", "grid"),
        check_vma=False,
    )
```

profile of v0, /device:TPU:1, one launch (start us, length us, event | category | flops | bytes accessed | tf_op | source)
XLA Modules:
  0.0 252.1 jit_solution(6418877580718086313)
XLA Ops:
  0.7 7.4 %route.1 = (s32[8,128]{1,0:T(8,128)S(1)}, s32[8,256]{1,0:T(8,128)S(1)}, s32[8,256]{1,0:T(8,128)S(1)}, s32[1]{0:T(128)}) custom-call(s32[1]{0:T(128)} %bitcast.3.me_ref, s32[8,256]{1,0:T(8,128)S(1)} %reshape.87.pair_ref, s32[3,512]{1,0:T(4,128)} %bitcast.34), custom_call_target="tpu_custom_call" | custom-call | flops 10000000 | bytes 1000000 | tf_op jit(solution)/shard_map/route/pallas_call | solution.py:201
  8.7 243.2 %conditional.4 = (f32[128,4096]{1,0:T(8,128)}) conditional(s32[]{:T(128)} %bitcast.6, (s32[1]{0:T(128)}, s32[256,4,2]{0,2,1:T(2,128)}, f32[128,4096]{1,0:T(8,128)}, s32[512,3]{0,1:T(4,128)}, s32[1]{0:T(128)}, /*index=5*/s32[8,128]{1,0:T(8,128)S(1)}, s32[8,256]{1,0:T(8,128)S(1)}, s32[8,256]{1,0:T(8,128)S(1)}) %tuple.65, (s32[512,3]{0,1:T(4,128)}, ...), branch_computations={%region_0.12_spmd, %region_12.13_spmd} | conditional | flops 111966608 | bytes 297047232 | solution.py:803
  8.9 3.6 %deal_near.3 = f32[64,56,128]{2,1,0:T(8,128)} custom-call(s32[8,128]{1,0:T(8,128)S(1)} %get-tuple-element.315.pos_ref, f32[128,4096]{1,0:T(8,128)} %get-tuple-element.319.orb_ref), custom_call_target="tpu_custom_call" | custom-call | flops 2000000 | bytes 10000000 | tf_op jit(solution)/shard_map/cond/branch_1_fun/deal_near/pallas_call | solution.py:317
  12.6 13.5 %all-to-all-start = ((f32[64,56,128]{2,1,0:T(8,128)}), f32[64,56,128]{2,1,0:T(8,128)}, u32[]{:S(2)}, u32[]{:S(2)}) async-start(f32[64,56,128]{2,1,0:T(8,128)} %deal_near.3), calls=%async_computation | async-start | bytes 3670016 | tf_op jit(solution)/shard_map/cond/branch_1_fun/all_to_all | solution.py:705
  26.4 1.3 send.3
  27.8 1.3 copy-done.2
  30.3 2.5 collective-permute-start.1
  33.9 15.1 %collective-permute-done.refs_1_ = f32[48,32,128]{2,1,0:T(8,128)S(1)} collective-permute-done((f32[48,32,128]{2,1,0:T(8,128)S(1)}, f32[48,32,128]{2,1,0:T(8,128)S(1)}, u32[]{:S(2)}, u32[]{:S(2)}) %collective-permute-start) | collective-permute-done | bytes 786464 | tf_op jit(solution)/shard_map/cond/branch_1_fun/ppermute | solution.py:701
  49.0 17.8 %collective-permute-done.1.refs_2_ = f32[48,32,128]{2,1,0:T(8,128)S(1)} collective-permute-done((f32[48,32,128]{2,1,0:T(8,128)S(1)}, f32[48,32,128]{2,1,0:T(8,128)S(1)}, u32[]{:S(2)}, u32[]{:S(2)}) %collective-permute-start.1) | collective-permute-done | bytes 786464 | tf_op jit(solution)/shard_map/cond/branch_1_fun/ppermute | solution.py:701
  67.7 4.6 %deal_far.7 = f32[64,56,128]{2,1,0:T(8,128)} custom-call(s32[8,128]{1,0:T(8,128)S(1)} %get-tuple-element.315.pos_ref, f32[128,32,128]{2,1,0:T(8,128)} %bitcast.28, f32[48,32,128]{2,1,0:T(8,128)} %copy-done.12, f32[48,32,128]{2,1,0:T(8,128)} %copy-done.13, f32[48,32,128]{2,1,0:T(8,128)} %collective-permute-done.2.refs_3_), custom_call_target="tpu_custom_call" | custom-call | bytes 12000000 | tf_op jit(solution)/shard_map/cond/branch_1_fun/deal_far/pallas_call | solution.py:356
  72.3 11.2 %all-to-all-start.1 = ((f32[64,56,128]{2,1,0:T(8,128)}), f32[64,56,128]{2,1,0:T(8,128)S(1)}, u32[]{:S(2)}, u32[]{:S(2)}) async-start(f32[64,56,128]{2,1,0:T(8,128)} %deal_far.7), calls=%async_computation.1 | async-start | bytes 3670016 | tf_op jit(solution)/shard_map/cond/branch_1_fun/all_to_all | solution.py:705
  83.9 45.0 %all-to-all-done.1.far_ref = f32[64,56,128]{2,1,0:T(8,128)S(1)} async-done(((f32[64,56,128]{2,1,0:T(8,128)}), f32[64,56,128]{2,1,0:T(8,128)S(1)}, u32[]{:S(2)}, u32[]{:S(2)}) %all-to-all-start.1) | async-done | bytes 1835040 | tf_op jit(solution)/shard_map/cond/branch_1_fun/all_to_all | solution.py:705
  129.0 12.8 %solve.5 = (f32[64,56,128]{2,1,0:T(8,128)S(1)}, f32[64,56,128]{2,1,0:T(8,128)S(1)}) custom-call(s32[1]{0:T(128)} %get-tuple-element.317.place_ref, s32[8,128]{1,0:T(8,128)S(1)} %get-tuple-element.315.pos_ref, s32[1536]{0:T(1024)S(1)} %reshape.84.anchor_ref, f32[64,56,128]{2,1,0:T(8,128)} %all-to-all-done.near_ref, f32[64,56,128]{2,1,0:T(8,128)S(1)} %all-to-all-done.1.far_ref), custom_call_target="tpu_custom_call" | custom-call | flops 100000000 | bytes 30000000 | tf_op jit(solution)/shard_map/cond/branch_1_fun/solve/pallas_call | solution.py:554
  141.8 51.4 %all_to_all.42.terms_ref.table_ref = f32[64,56,128]{2,1,0:T(8,128)S(1)} all-to-all(f32[64,56,128]{2,1,0:T(8,128)S(1)} %get-tuple-element.323), channel_id=1, replica_groups=mesh['grp'=4,'grid'=64] {'grid'}, dimensions={0} | all-to-all | bytes 3670016 | tf_op jit(solution)/shard_map/cond/branch_1_fun/all_to_all | solution.py:705
  193.2 6.2 %all-to-all-start.3 = ((f32[64,56,128]{2,1,0:T(8,128)}), f32[64,56,128]{2,1,0:T(8,128)}, u32[]{:S(2)}, u32[]{:S(2)}) async-start(f32[64,56,128]{2,1,0:T(8,128)} %copy-done.5), calls=%async_computation.3 | async-start | bytes 3670016 | tf_op jit(solution)/shard_map/cond/branch_1_fun/all_to_all | solution.py:705
  199.4 1.8 back.3
  201.3 1.2 collective-permute-start.3
  203.8 2.6 %add_far.3.sum_ref = f32[130,32,128]{2,1,0:T(8,128)S(1)} custom-call(s32[8,128]{1,0:T(8,128)S(1)} %get-tuple-element.315.pos_ref, f32[64,56,128]{2,1,0:T(8,128)S(1)} %all_to_all.42.terms_ref.table_ref), custom_call_target="tpu_custom_call" | custom-call | flops 2000000 | bytes 4000000 | tf_op jit(solution)/shard_map/cond/branch_1_fun/add_far/pallas_call | solution.py:595
  206.4 1.4 copy-done.4
  207.7 12.3 %collective-permute-done.3.refs_0_ = f32[48,32,128]{2,1,0:T(8,128)S(1)} collective-permute-done((f32[48,32,128]{2,1,0:T(8,128)S(1)}, f32[48,32,128]{2,1,0:T(8,128)S(1)}, u32[]{:S(2)}, u32[]{:S(2)}) %collective-permute-start.3) | collective-permute-done | bytes 786464 | tf_op jit(solution)/shard_map/cond/branch_1_fun/ppermute | solution.py:701
  220.0 2.4 collective-permute-done.4.refs_1_
  223.4 17.0 %collective-permute-done.5.refs_2_ = f32[48,32,128]{2,1,0:T(8,128)} collective-permute-done((f32[48,32,128]{2,1,0:T(8,128)S(1)}, f32[48,32,128]{2,1,0:T(8,128)}, u32[]{:S(2)}, u32[]{:S(2)}) %collective-permute-start.5) | collective-permute-done | bytes 786464 | tf_op jit(solution)/shard_map/cond/branch_1_fun/ppermute | solution.py:701
  240.4 6.6 %add_arrived.3.sum_ref = f32[130,32,128]{2,1,0:T(8,128)} custom-call(s32[8,256]{1,0:T(8,128)S(1)} %get-tuple-element.316.idx_ref.slot_ref, f32[130,32,128]{2,1,0:T(8,128)} %copy-done.4, f32[48,32,128]{2,1,0:T(8,128)} %copy-done.9, f32[48,32,128]{2,1,0:T(8,128)} %copy-done.11, f32[48,32,128]{2,1,0:T(8,128)} %collective-permute-done.5.refs_2_), custom_call_target="tpu_custom_call" | custom-call | flops 2000000 | bytes 6000000 | tf_op jit(solution)/shard_map/cond/branch_1_fun/add_arrived/pallas_call | solution.py:628
  247.0 4.9 %add_near.3 = f32[128,4096]{1,0:T(8,128)} custom-call(s32[8,128]{1,0:T(8,128)S(1)} %get-tuple-element.315.pos_ref, f32[130,32,128]{2,1,0:T(8,128)} %add_arrived.3.sum_ref, f32[64,56,128]{2,1,0:T(8,128)} %all-to-all-done.3.terms_ref), custom_call_target="tpu_custom_call" | custom-call | flops 2000000 | bytes 10000000 | tf_op jit(solution)/shard_map/cond/branch_1_fun/add_near/pallas_call | solution.py:680
  (27 shorter events, 7.0 us)
Async XLA Ops:
  12.6 13.5 %copy-start.7 = (f32[128,4096]{1,0:T(8,128)S(1)}, f32[128,4096]{1,0:T(8,128)}, u32[]{:S(2)}) copy-start(f32[128,4096]{1,0:T(8,128)} %get-tuple-element.319.orb_ref) | copy-start | bytes 6291460 | tf_op jit(solution)/shard_map/cond
  12.6 59.7 %all-to-all-start = ((f32[64,56,128]{2,1,0:T(8,128)}), f32[64,56,128]{2,1,0:T(8,128)}, u32[]{:S(2)}, u32[]{:S(2)}) async-start(f32[64,56,128]{2,1,0:T(8,128)} %deal_near.3), calls=%async_computation | async-start | bytes 3670016 | tf_op jit(solution)/shard_map/cond/branch_1_fun/all_to_all | solution.py:705
  27.8 1.3 copy-start.2
  29.1 19.9 %collective-permute-start = (f32[48,32,128]{2,1,0:T(8,128)S(1)}, f32[48,32,128]{2,1,0:T(8,128)S(1)}, u32[]{:S(2)}, u32[]{:S(2)}) collective-permute-start(f32[48,32,128]{2,1,0:T(8,128)S(1)} %get-tuple-element.320), channel_id=1, source_target_pairs={{0,64},{64,128},{128,192},{192,0},{1,65},{65,129},{129,193},{193,1... | collective-permute-start | bytes 2359304 | tf_op jit(solution)/shard_map/cond/branch_1_fun/ppermute | solution.py:701
  30.3 36.5 %collective-permute-start.1 = (f32[48,32,128]{2,1,0:T(8,128)S(1)}, f32[48,32,128]{2,1,0:T(8,128)S(1)}, u32[]{:S(2)}, u32[]{:S(2)}) collective-permute-start(f32[48,32,128]{2,1,0:T(8,128)S(1)} %get-tuple-element.321), channel_id=1, source_target_pairs={{0,128},{64,192},{128,0},{192,64},{1,129},{65,193},{129,1},{193,65... | collective-permute-start | bytes 2359304 | tf_op jit(solution)/shard_map/cond/branch_1_fun/ppermute | solution.py:701
  32.8 35.0 %collective-permute-start.2 = (f32[48,32,128]{2,1,0:T(8,128)S(1)}, f32[48,32,128]{2,1,0:T(8,128)}, u32[]{:S(2)}, u32[]{:S(2)}) collective-permute-start(f32[48,32,128]{2,1,0:T(8,128)S(1)} %get-tuple-element.322), channel_id=1, source_target_pairs={{0,192},{64,0},{128,64},{192,128},{1,193},{65,1},{129,65},{193,129... | collective-permute-start | bytes 2359304 | tf_op jit(solution)/shard_map/cond/branch_1_fun/ppermute | solution.py:701
  49.0 17.8 %copy-start.12 = (f32[48,32,128]{2,1,0:T(8,128)}, f32[48,32,128]{2,1,0:T(8,128)S(1)}, u32[]{:S(2)}) copy-start(f32[48,32,128]{2,1,0:T(8,128)S(1)} %collective-permute-done.refs_1_) | copy-start | bytes 2359300 | tf_op jit(solution)/shard_map/cond
  66.9 0.9 copy-start.13
  72.3 11.3 %copy-start.14 = (s32[512,3]{0,1:T(4,128)S(1)}, s32[512,3]{0,1:T(4,128)}, u32[]{:S(2)}) copy-start(s32[512,3]{0,1:T(4,128)} %get-tuple-element.368) | copy-start | bytes 18436 | tf_op jit(solution)/shard_map/cond
  72.3 56.7 %all-to-all-start.1 = ((f32[64,56,128]{2,1,0:T(8,128)}), f32[64,56,128]{2,1,0:T(8,128)S(1)}, u32[]{:S(2)}, u32[]{:S(2)}) async-start(f32[64,56,128]{2,1,0:T(8,128)} %deal_far.7), calls=%async_computation.1 | async-start | bytes 3670016 | tf_op jit(solution)/shard_map/cond/branch_1_fun/all_to_all | solution.py:705
  141.8 51.4 %copy-start.5 = (f32[64,56,128]{2,1,0:T(8,128)}, f32[64,56,128]{2,1,0:T(8,128)S(1)}, u32[]{:S(2)}) copy-start(f32[64,56,128]{2,1,0:T(8,128)S(1)} %get-tuple-element.328) | copy-start | bytes 5505028 | tf_op jit(solution)/shard_map/cond
  193.2 53.9 %all-to-all-start.3 = ((f32[64,56,128]{2,1,0:T(8,128)}), f32[64,56,128]{2,1,0:T(8,128)}, u32[]{:S(2)}, u32[]{:S(2)}) async-start(f32[64,56,128]{2,1,0:T(8,128)} %copy-done.5), calls=%async_computation.3 | async-start | bytes 3670016 | tf_op jit(solution)/shard_map/cond/branch_1_fun/all_to_all | solution.py:705
  201.3 18.8 %collective-permute-start.3 = (f32[48,32,128]{2,1,0:T(8,128)S(1)}, f32[48,32,128]{2,1,0:T(8,128)S(1)}, u32[]{:S(2)}, u32[]{:S(2)}) collective-permute-start(f32[48,32,128]{2,1,0:T(8,128)S(1)} %get-tuple-element.325), channel_id=1, source_target_pairs={{0,192},{64,0},{128,64},{192,128},{1,193},{65,1},{129,65},{193,129... | collective-permute-start | bytes 2359304 | tf_op jit(solution)/shard_map/cond/branch_1_fun/ppermute | solution.py:701
  202.5 19.9 %collective-permute-start.4 = (f32[48,32,128]{2,1,0:T(8,128)S(1)}, f32[48,32,128]{2,1,0:T(8,128)S(1)}, u32[]{:S(2)}, u32[]{:S(2)}) collective-permute-start(f32[48,32,128]{2,1,0:T(8,128)S(1)} %get-tuple-element.326), channel_id=1, source_target_pairs={{0,128},{64,192},{128,0},{192,64},{1,129},{65,193},{129,1},{193,65... | collective-permute-start | bytes 2359304 | tf_op jit(solution)/shard_map/cond/branch_1_fun/ppermute | solution.py:701
  203.4 37.0 %collective-permute-start.5 = (f32[48,32,128]{2,1,0:T(8,128)S(1)}, f32[48,32,128]{2,1,0:T(8,128)}, u32[]{:S(2)}, u32[]{:S(2)}) collective-permute-start(f32[48,32,128]{2,1,0:T(8,128)S(1)} %get-tuple-element.327), channel_id=1, source_target_pairs={{0,64},{64,128},{128,192},{192,0},{1,65},{65,129},{129,193},{193,1... | collective-permute-start | bytes 2359304 | tf_op jit(solution)/shard_map/cond/branch_1_fun/ppermute | solution.py:701
  206.4 1.4 copy-start.4
  220.0 2.4 copy-start.9
  222.4 1.0 copy-start.11
where the time goes:
time: 253 us; the launch traced here: 252 us
  waiting for transfers between devices  110 us (43%)
  blocking collectives  51.4 us (20%)
  Pallas kernels  45.6 us (18%)
  starting transfers between devices  38.3 us (15%)
  local copies, waits for them, and re-layouts  5.96 us (2%)
    ppermute x6, waiting for transfers between devices, turned(): lax.ppermute(x, 'grp', [(g, (g + shift) % groups) for g in range(groups)])  64.6 us
    all_to_all x1, blocking collectives, exchanged(): return lax.all_to_all(planes, 'grid', 0, 0, tiled=True)  51.4 us
    all_to_all x3, waiting for transfers between devices, exchanged(): return lax.all_to_all(planes, 'grid', 0, 0, tiled=True)  45 us
    all_to_all x3, starting transfers between devices, exchanged(): return lax.all_to_all(planes, 'grid', 0, 0, tiled=True)  30.9 us
    pallas_call x1, Pallas kernels, solve(): pl.pallas_call(pair_kernel, out_shape=[jax.ShapeDtypeStruct(near.shape, j...  12.8 us
    pallas_call x1, Pallas kernels, route(): pl.pallas_call(route_kernel, out_shape=[jax.ShapeDtypeStruct((8, 128), jn...  7.35 us
    ppermute x6, starting transfers between devices, turned(): lax.ppermute(x, 'grp', [(g, (g + shift) % groups) for g in range(groups)])  7.31 us
    pallas_call x1, Pallas kernels, add_arrived(): pl.pallas_call(add_arrived_kernel, out_shape=jax.ShapeDtypeStruct(summed....  6.62 us
  transfers between devices with their start and end apart: 9, of which 6 were waited for; matrix products, arithmetic and copies ran while one was open for 0% of the time, Pallas kernels for 6%

commit v1 on v0

--- a/solution.py
+++ b/solution.py
@@ -359,7 +359,7 @@
         in_specs=[pl.BlockSpec(memory_space=pltpu.SMEM)] + [pl.BlockSpec(memory_space=pl.ANY)] * len(parts),
         out_specs=pl.BlockSpec(memory_space=pltpu.VMEM),
         scratch_shapes=[pltpu.VMEM((rows + 2, ROWS, 128), jnp.float32), pltpu.SemaphoreType.DMA((len(parts),))],
-        compiler_params=pltpu.CompilerParams(vmem_limit_bytes=63 << 20),
+        compiler_params=pltpu.CompilerParams(vmem_limit_bytes=32 << 20),
         cost_estimate=pl.CostEstimate(flops=0, bytes_accessed=12_000_000, transcendentals=0),
         name="deal_far",
     )(pos, *parts)
@@ -631,7 +631,7 @@
         in_specs=[smem, pl.BlockSpec(memory_space=pl.ANY)] + [vmem] * 3,
         out_specs=vmem,
         scratch_shapes=[pltpu.SemaphoreType.DMA],
-        compiler_params=pltpu.CompilerParams(vmem_limit_bytes=63 << 20),
+        compiler_params=pltpu.CompilerParams(vmem_limit_bytes=24 << 20),
         cost_estimate=pl.CostEstimate(flops=2_000_000, bytes_accessed=6_000_000, transcendentals=0),
         name="add_arrived",
     )(slot, summed, *from_groups)

time: 253 us -> 249 us (0.984)
  Pallas kernels: 45.6 us -> 38.9 us
  waiting for transfers between devices: 110 us -> 114 us
    pallas_call x1, Pallas kernels: 6.62 us -> 2.93 us  [add_arrived(): pl.pallas_call(add_arrived_kernel, out_shape=jax.ShapeDtypeStruct(summed....]
    pallas_call x1, Pallas kernels: 4.55 us -> 1.36 us  [deal_far(): pl.pallas_call(functools.partial(deal_far_kernel, row), out_shape=jax.Sha...]
  transfers between devices with their start and end apart: 9 -> 9, of which waited for: 6 -> 7; matrix products, arithmetic and copies ran while one was open for 0% -> 1% of each run, Pallas kernels for 6% -> 4%
where the time goes in v1:
time: 249 us; the launch traced here: 248 us
  waiting for transfers between devices  114 us (46%)
  blocking collectives  51.3 us (21%)
  Pallas kernels  38.9 us (16%)
  starting transfers between devices  37.4 us (15%)
  local copies, waits for them, and re-layouts  5.59 us (2%)
    ppermute x6, waiting for transfers between devices, turned(): lax.ppermute(x, 'grp', [(g, (g + shift) % groups) for g in range(groups)])  67 us
    all_to_all x1, blocking collectives, exchanged(): return lax.all_to_all(planes, 'grid', 0, 0, tiled=True)  51.3 us
    all_to_all x3, waiting for transfers between devices, exchanged(): return lax.all_to_all(planes, 'grid', 0, 0, tiled=True)  46.7 us
    all_to_all x3, starting transfers between devices, exchanged(): return lax.all_to_all(planes, 'grid', 0, 0, tiled=True)  29.3 us
    pallas_call x1, Pallas kernels, solve(): pl.pallas_call(pair_kernel, out_shape=[jax.ShapeDtypeStruct(near.shape, j...  13 us
    ppermute x6, starting transfers between devices, turned(): lax.ppermute(x, 'grp', [(g, (g + shift) % groups) for g in range(groups)])  8.15 us
    pallas_call x1, Pallas kernels, route(): pl.pallas_call(route_kernel, out_shape=[jax.ShapeDtypeStruct((8, 128), jn...  7.35 us
  transfers between devices with their start and end apart: 9, of which 7 were waited for; matrix products, arithmetic and copies ran while one was open for 1% of the time, Pallas kernels for 4%

profile of v1, /device:TPU:1, one launch (start us, length us, event | category | flops | bytes accessed | tf_op | source)
XLA Modules:
  0.0 248.2 jit_solution(10558515761709859684)
XLA Ops:
  0.7 7.4 %route.1 = (s32[8,128]{1,0:T(8,128)S(1)}, s32[8,256]{1,0:T(8,128)S(1)}, s32[8,256]{1,0:T(8,128)S(1)}, s32[1]{0:T(128)}) custom-call(s32[1]{0:T(128)} %bitcast.3.me_ref, s32[8,256]{1,0:T(8,128)S(1)} %reshape.87.pair_ref, s32[3,512]{1,0:T(4,128)} %bitcast.34), custom_call_target="tpu_custom_call" | custom-call | flops 10000000 | bytes 1000000 | tf_op jit(solution)/shard_map/route/pallas_call | solution.py:201
  8.7 239.2 %conditional.4 = (f32[128,4096]{1,0:T(8,128)}) conditional(s32[]{:T(128)} %bitcast.6, (s32[1]{0:T(128)}, s32[256,4,2]{0,2,1:T(2,128)}, f32[128,4096]{1,0:T(8,128)}, s32[512,3]{0,1:T(4,128)}, s32[1]{0:T(128)}, /*index=5*/s32[8,128]{1,0:T(8,128)S(1)}, s32[8,256]{1,0:T(8,128)S(1)}, s32[8,256]{1,0:T(8,128)S(1)}) %tuple.65, (s32[512,3]{0,1:T(4,128)}, ...), branch_computations={%region_0.12_spmd, %region_12.13_spmd} | conditional | flops 111966608 | bytes 313824512 | solution.py:803
  9.0 3.6 %deal_near.3 = f32[64,56,128]{2,1,0:T(8,128)} custom-call(s32[8,128]{1,0:T(8,128)S(1)} %get-tuple-element.315.pos_ref, f32[128,4096]{1,0:T(8,128)} %get-tuple-element.319.orb_ref), custom_call_target="tpu_custom_call" | custom-call | flops 2000000 | bytes 10000000 | tf_op jit(solution)/shard_map/cond/branch_1_fun/deal_near/pallas_call | solution.py:317
  12.6 13.2 %all-to-all-start = ((f32[64,56,128]{2,1,0:T(8,128)}), f32[64,56,128]{2,1,0:T(8,128)S(1)}, u32[]{:S(2)}, u32[]{:S(2)}) async-start(f32[64,56,128]{2,1,0:T(8,128)} %deal_near.3), calls=%async_computation | async-start | bytes 3670016 | tf_op jit(solution)/shard_map/cond/branch_1_fun/all_to_all | solution.py:705
  25.8 2.0 copy.20
  30.4 2.5 collective-permute-start.1
  34.0 15.1 %collective-permute-done.refs_1_ = f32[48,32,128]{2,1,0:T(8,128)S(1)} collective-permute-done((f32[48,32,128]{2,1,0:T(8,128)S(1)}, f32[48,32,128]{2,1,0:T(8,128)S(1)}, u32[]{:S(2)}, u32[]{:S(2)}) %collective-permute-start) | collective-permute-done | bytes 786464 | tf_op jit(solution)/shard_map/cond/branch_1_fun/ppermute | solution.py:701
  49.0 17.8 %collective-permute-done.1.refs_2_ = f32[48,32,128]{2,1,0:T(8,128)S(1)} collective-permute-done((f32[48,32,128]{2,1,0:T(8,128)S(1)}, f32[48,32,128]{2,1,0:T(8,128)S(1)}, u32[]{:S(2)}, u32[]{:S(2)}) %collective-permute-start.1) | collective-permute-done | bytes 786464 | tf_op jit(solution)/shard_map/cond/branch_1_fun/ppermute | solution.py:701
  66.9 1.4 deal_far.7
  69.5 1.7 all-to-all-done.near_ref
  71.2 9.9 %all-to-all-start.1 = ((f32[64,56,128]{2,1,0:T(8,128)}), f32[64,56,128]{2,1,0:T(8,128)}, u32[]{:S(2)}, u32[]{:S(2)}) async-start(f32[64,56,128]{2,1,0:T(8,128)} %copy-done.3), calls=%async_computation.1 | async-start | bytes 3670016 | tf_op jit(solution)/shard_map/cond/branch_1_fun/all_to_all | solution.py:705
  81.4 45.0 %all-to-all-done.1.far_ref = f32[64,56,128]{2,1,0:T(8,128)} async-done(((f32[64,56,128]{2,1,0:T(8,128)}), f32[64,56,128]{2,1,0:T(8,128)}, u32[]{:S(2)}, u32[]{:S(2)}) %all-to-all-start.1) | async-done | bytes 1835040 | tf_op jit(solution)/shard_map/cond/branch_1_fun/all_to_all | solution.py:705
  126.4 13.0 %solve.5 = (f32[64,56,128]{2,1,0:T(8,128)S(1)}, f32[64,56,128]{2,1,0:T(8,128)S(1)}) custom-call(s32[1]{0:T(128)} %get-tuple-element.317.place_ref, s32[8,128]{1,0:T(8,128)S(1)} %get-tuple-element.315.pos_ref, s32[1536]{0:T(1024)S(1)} %reshape.84.anchor_ref, f32[64,56,128]{2,1,0:T(8,128)S(1)} %all-to-all-done.near_ref, f32[64,56,128]{2,1,0:T(8,128)} %all-to-all-done.1.far_ref), custom_call_target="tpu_custom_call" | custom-call | flops 100000000 | bytes 30000000 | tf_op jit(solution)/shard_map/cond/branch_1_fun/solve/pallas_call | solution.py:554
  139.4 51.3 %all_to_all.42.terms_ref.table_ref = f32[64,56,128]{2,1,0:T(8,128)S(1)} all-to-all(f32[64,56,128]{2,1,0:T(8,128)S(1)} %get-tuple-element.323), channel_id=1, replica_groups=mesh['grp'=4,'grid'=64] {'grid'}, dimensions={0} | all-to-all | bytes 3670016 | tf_op jit(solution)/shard_map/cond/branch_1_fun/all_to_all | solution.py:705
  190.7 6.2 %all-to-all-start.3 = ((f32[64,56,128]{2,1,0:T(8,128)}), f32[64,56,128]{2,1,0:T(8,128)}, u32[]{:S(2)}, u32[]{:S(2)}) async-start(f32[64,56,128]{2,1,0:T(8,128)} %copy-done.4), calls=%async_computation.3 | async-start | bytes 3670016 | tf_op jit(solution)/shard_map/cond/branch_1_fun/all_to_all | solution.py:705
  197.0 1.8 back.3
  198.8 2.1 collective-permute-start.3
  202.1 2.6 %add_far.3.sum_ref = f32[130,32,128]{2,1,0:T(8,128)S(1)} custom-call(s32[8,128]{1,0:T(8,128)S(1)} %get-tuple-element.315.pos_ref, f32[64,56,128]{2,1,0:T(8,128)S(1)} %all_to_all.42.terms_ref.table_ref), custom_call_target="tpu_custom_call" | custom-call | flops 2000000 | bytes 4000000 | tf_op jit(solution)/shard_map/cond/branch_1_fun/add_far/pallas_call | solution.py:595
  204.7 12.9 %collective-permute-done.3.refs_0_ = f32[48,32,128]{2,1,0:T(8,128)S(1)} collective-permute-done((f32[48,32,128]{2,1,0:T(8,128)S(1)}, f32[48,32,128]{2,1,0:T(8,128)S(1)}, u32[]{:S(2)}, u32[]{:S(2)}) %collective-permute-start.3) | collective-permute-done | bytes 786464 | tf_op jit(solution)/shard_map/cond/branch_1_fun/ppermute | solution.py:701
  217.6 3.2 %collective-permute-done.4.refs_1_ = f32[48,32,128]{2,1,0:T(8,128)S(1)} collective-permute-done((f32[48,32,128]{2,1,0:T(8,128)S(1)}, f32[48,32,128]{2,1,0:T(8,128)S(1)}, u32[]{:S(2)}, u32[]{:S(2)}) %collective-permute-start.4) | collective-permute-done | bytes 786464 | tf_op jit(solution)/shard_map/cond/branch_1_fun/ppermute | solution.py:701
  220.8 18.0 %collective-permute-done.5.refs_2_ = f32[48,32,128]{2,1,0:T(8,128)S(1)} collective-permute-done((f32[48,32,128]{2,1,0:T(8,128)S(1)}, f32[48,32,128]{2,1,0:T(8,128)S(1)}, u32[]{:S(2)}, u32[]{:S(2)}) %collective-permute-start.5) | collective-permute-done | bytes 786464 | tf_op jit(solution)/shard_map/cond/branch_1_fun/ppermute | solution.py:701
  238.8 2.9 %add_arrived.3.sum_ref = f32[130,32,128]{2,1,0:T(8,128)S(1)} custom-call(s32[8,256]{1,0:T(8,128)S(1)} %get-tuple-element.316.idx_ref.slot_ref, f32[130,32,128]{2,1,0:T(8,128)S(1)} %add_far.3.sum_ref, f32[48,32,128]{2,1,0:T(8,128)S(1)} %collective-permute-done.3.refs_0_, f32[48,32,128]{2,1,0:T(8,128)S(1)} %collective-permute-done.4.refs_1_, ...), custom_call_target="tpu_custom_call" | custom-call | flops 2000000 | bytes 6000000 | tf_op jit(solution)/shard_map/cond/branch_1_fun/add_arrived/pallas_call | solution.py:628
  241.7 1.4 copy-done.1
  243.1 4.9 %add_near.3 = f32[128,4096]{1,0:T(8,128)} custom-call(s32[8,128]{1,0:T(8,128)S(1)} %get-tuple-element.315.pos_ref, f32[130,32,128]{2,1,0:T(8,128)} %copy-done.1, f32[64,56,128]{2,1,0:T(8,128)} %all-to-all-done.3.terms_ref), custom_call_target="tpu_custom_call" | custom-call | flops 2000000 | bytes 10000000 | tf_op jit(solution)/shard_map/cond/branch_1_fun/add_near/pallas_call | solution.py:680
  (17 shorter events, 7.3 us)
Async XLA Ops:
  12.6 58.6 %all-to-all-start = ((f32[64,56,128]{2,1,0:T(8,128)}), f32[64,56,128]{2,1,0:T(8,128)S(1)}, u32[]{:S(2)}, u32[]{:S(2)}) async-start(f32[64,56,128]{2,1,0:T(8,128)} %deal_near.3), calls=%async_computation | async-start | bytes 3670016 | tf_op jit(solution)/shard_map/cond/branch_1_fun/all_to_all | solution.py:705
  29.1 19.9 %collective-permute-start = (f32[48,32,128]{2,1,0:T(8,128)S(1)}, f32[48,32,128]{2,1,0:T(8,128)S(1)}, u32[]{:S(2)}, u32[]{:S(2)}) collective-permute-start(f32[48,32,128]{2,1,0:T(8,128)S(1)} %get-tuple-element.320), channel_id=1, source_target_pairs={{0,64},{64,128},{128,192},{192,0},{1,65},{65,129},{129,193},{193,1... | collective-permute-start | bytes 2359304 | tf_op jit(solution)/shard_map/cond/branch_1_fun/ppermute | solution.py:701
  30.4 36.5 %collective-permute-start.1 = (f32[48,32,128]{2,1,0:T(8,128)S(1)}, f32[48,32,128]{2,1,0:T(8,128)S(1)}, u32[]{:S(2)}, u32[]{:S(2)}) collective-permute-start(f32[48,32,128]{2,1,0:T(8,128)S(1)} %get-tuple-element.321), channel_id=1, source_target_pairs={{0,128},{64,192},{128,0},{192,64},{1,129},{65,193},{129,1},{193,65... | collective-permute-start | bytes 2359304 | tf_op jit(solution)/shard_map/cond/branch_1_fun/ppermute | solution.py:701
  32.8 34.1 %collective-permute-start.2 = (f32[48,32,128]{2,1,0:T(8,128)S(1)}, f32[48,32,128]{2,1,0:T(8,128)S(1)}, u32[]{:S(2)}, u32[]{:S(2)}) collective-permute-start(f32[48,32,128]{2,1,0:T(8,128)S(1)} %get-tuple-element.322), channel_id=1, source_target_pairs={{0,192},{64,0},{128,64},{192,128},{1,193},{65,1},{129,65},{193,129... | collective-permute-start | bytes 2359304 | tf_op jit(solution)/shard_map/cond/branch_1_fun/ppermute | solution.py:701
  68.2 1.2 copy-start.3
  69.5 11.6 %copy-start.9 = (s32[512,3]{0,1:T(4,128)S(1)}, s32[512,3]{0,1:T(4,128)}, u32[]{:S(2)}) copy-start(s32[512,3]{0,1:T(4,128)} %get-tuple-element.368) | copy-start | bytes 18436 | tf_op jit(solution)/shard_map/cond
  71.2 55.2 %all-to-all-start.1 = ((f32[64,56,128]{2,1,0:T(8,128)}), f32[64,56,128]{2,1,0:T(8,128)}, u32[]{:S(2)}, u32[]{:S(2)}) async-start(f32[64,56,128]{2,1,0:T(8,128)} %copy-done.3), calls=%async_computation.1 | async-start | bytes 3670016 | tf_op jit(solution)/shard_map/cond/branch_1_fun/all_to_all | solution.py:705
  139.4 51.3 %copy-start.4 = (f32[64,56,128]{2,1,0:T(8,128)}, f32[64,56,128]{2,1,0:T(8,128)S(1)}, u32[]{:S(2)}) copy-start(f32[64,56,128]{2,1,0:T(8,128)S(1)} %get-tuple-element.328) | copy-start | bytes 5505028 | tf_op jit(solution)/shard_map/cond
  190.7 52.4 %all-to-all-start.3 = ((f32[64,56,128]{2,1,0:T(8,128)}), f32[64,56,128]{2,1,0:T(8,128)}, u32[]{:S(2)}, u32[]{:S(2)}) async-start(f32[64,56,128]{2,1,0:T(8,128)} %copy-done.4), calls=%async_computation.3 | async-start | bytes 3670016 | tf_op jit(solution)/shard_map/cond/branch_1_fun/all_to_all | solution.py:705
  198.8 18.8 %collective-permute-start.3 = (f32[48,32,128]{2,1,0:T(8,128)S(1)}, f32[48,32,128]{2,1,0:T(8,128)S(1)}, u32[]{:S(2)}, u32[]{:S(2)}) collective-permute-start(f32[48,32,128]{2,1,0:T(8,128)S(1)} %get-tuple-element.325), channel_id=1, source_target_pairs={{0,192},{64,0},{128,64},{192,128},{1,193},{65,1},{129,65},{193,129... | collective-permute-start | bytes 2359304 | tf_op jit(solution)/shard_map/cond/branch_1_fun/ppermute | solution.py:701
  200.9 19.9 %collective-permute-start.4 = (f32[48,32,128]{2,1,0:T(8,128)S(1)}, f32[48,32,128]{2,1,0:T(8,128)S(1)}, u32[]{:S(2)}, u32[]{:S(2)}) collective-permute-start(f32[48,32,128]{2,1,0:T(8,128)S(1)} %get-tuple-element.326), channel_id=1, source_target_pairs={{0,128},{64,192},{128,0},{192,64},{1,129},{65,193},{129,1},{193,65... | collective-permute-start | bytes 2359304 | tf_op jit(solution)/shard_map/cond/branch_1_fun/ppermute | solution.py:701
  201.7 37.1 %collective-permute-start.5 = (f32[48,32,128]{2,1,0:T(8,128)S(1)}, f32[48,32,128]{2,1,0:T(8,128)S(1)}, u32[]{:S(2)}, u32[]{:S(2)}) collective-permute-start(f32[48,32,128]{2,1,0:T(8,128)S(1)} %get-tuple-element.327), channel_id=1, source_target_pairs={{0,64},{64,128},{128,192},{192,0},{1,65},{65,129},{129,193},{193,1... | collective-permute-start | bytes 2359304 | tf_op jit(solution)/shard_map/cond/branch_1_fun/ppermute | solution.py:701
  241.7 1.4 copy-start.1

commit v2 on v1

--- a/solution.py
+++ b/solution.py
@@ -12,7 +12,7 @@
 ITERS = 3
 ROWS = B * B // 128
 KEEP = 48
-UNROLL = 16
+UNROLL = 32
 TRIMMED = 56
 
 
@@ -613,14 +613,10 @@
     def there(k, carry):
         for d, ref in enumerate(from_groups):
             at = d * KEEP + k
-
-            @pl.when(slot_ref[2, at] == 1)
-            def _(at=at, ref=ref):
-                add_lines(total, slot_ref[3, at], ref[k])
-
+            add_lines(total, slot_ref[3, at], jnp.where(slot_ref[2, at] == 1, ref[k], 0.0))
         return carry
 
-    lax.fori_loop(0, KEEP, there, 0)
+    lax.fori_loop(0, KEEP, there, 0, unroll=2)
 
 
 def add_arrived(slot, summed, from_groups):

time: 249 us -> 247 us (level)
  transfers between devices with their start and end apart: 9 -> 9, of which waited for: 7 -> 8; matrix products, arithmetic and copies ran while one was open for 1% -> 1% of each run, Pallas kernels for 4% -> 3%
where the time goes in v2:
time: 247 us
  waiting for transfers between devices  114 us (46%)
  blocking collectives  51.3 us (21%)
  starting transfers between devices  37.5 us (15%)
  Pallas kernels  37.1 us (15%)
  local copies, waits for them, and re-layouts  5.59 us (2%)
    ppermute x6, waiting for transfers between devices, turned(): lax.ppermute(x, 'grp', [(g, (g + shift) % groups) for g in range(groups)])  66.9 us
    all_to_all x1, blocking collectives, exchanged(): return lax.all_to_all(planes, 'grid', 0, 0, tiled=True)  51.3 us
    all_to_all x3, waiting for transfers between devices, exchanged(): return lax.all_to_all(planes, 'grid', 0, 0, tiled=True)  47 us
    all_to_all x3, starting transfers between devices, exchanged(): return lax.all_to_all(planes, 'grid', 0, 0, tiled=True)  29.3 us
    pallas_call x1, Pallas kernels, solve(): pl.pallas_call(pair_kernel, out_shape=[jax.ShapeDtypeStruct(near.shape, j...  12.3 us
    ppermute x6, starting transfers between devices, turned(): lax.ppermute(x, 'grp', [(g, (g + shift) % groups) for g in range(groups)])  8.27 us
    pallas_call x1, Pallas kernels, route(): pl.pallas_call(route_kernel, out_shape=[jax.ShapeDtypeStruct((8, 128), jn...  7.35 us
  transfers between devices with their start and end apart: 9, of which 8 were waited for; matrix products, arithmetic and copies ran while one was open for 1% of the time, Pallas kernels for 3%

profile of v2, /device:TPU:1, one launch (start us, length us, event | category | flops | bytes accessed | tf_op | source)
XLA Modules:
  0.0 246.6 jit_solution(12310680063031307319)
XLA Ops:
  0.7 7.4 %route.1 = (s32[8,128]{1,0:T(8,128)S(1)}, s32[8,256]{1,0:T(8,128)S(1)}, s32[8,256]{1,0:T(8,128)S(1)}, s32[1]{0:T(128)}) custom-call(s32[1]{0:T(128)} %bitcast.3.me_ref, s32[8,256]{1,0:T(8,128)S(1)} %reshape.87.pair_ref, s32[3,512]{1,0:T(4,128)} %bitcast.34), custom_call_target="tpu_custom_call" | custom-call | flops 10000000 | bytes 1000000 | tf_op jit(solution)/shard_map/route/pallas_call | solution.py:201
  8.7 237.7 %conditional.4 = (f32[128,4096]{1,0:T(8,128)}) conditional(s32[]{:T(128)} %bitcast.6, (s32[1]{0:T(128)}, s32[256,4,2]{0,2,1:T(2,128)}, f32[128,4096]{1,0:T(8,128)}, s32[512,3]{0,1:T(4,128)}, s32[1]{0:T(128)}, /*index=5*/s32[8,128]{1,0:T(8,128)S(1)}, s32[8,256]{1,0:T(8,128)S(1)}, s32[8,256]{1,0:T(8,128)S(1)}) %tuple.65, (s32[512,3]{0,1:T(4,128)}, ...), branch_computations={%region_0.12_spmd, %region_12.13_spmd} | conditional | flops 111966608 | bytes 313824512 | solution.py:799
  8.9 3.6 %deal_near.3 = f32[64,56,128]{2,1,0:T(8,128)} custom-call(s32[8,128]{1,0:T(8,128)S(1)} %get-tuple-element.315.pos_ref, f32[128,4096]{1,0:T(8,128)} %get-tuple-element.319.orb_ref), custom_call_target="tpu_custom_call" | custom-call | flops 2000000 | bytes 10000000 | tf_op jit(solution)/shard_map/cond/branch_1_fun/deal_near/pallas_call | solution.py:317
  12.5 13.2 %all-to-all-start = ((f32[64,56,128]{2,1,0:T(8,128)}), f32[64,56,128]{2,1,0:T(8,128)S(1)}, u32[]{:S(2)}, u32[]{:S(2)}) async-start(f32[64,56,128]{2,1,0:T(8,128)} %deal_near.3), calls=%async_computation | async-start | bytes 3670016 | tf_op jit(solution)/shard_map/cond/branch_1_fun/all_to_all | solution.py:701
  25.7 2.0 copy.20
  30.3 2.4 collective-permute-start.1
  33.9 15.1 %collective-permute-done.refs_1_ = f32[48,32,128]{2,1,0:T(8,128)S(1)} collective-permute-done((f32[48,32,128]{2,1,0:T(8,128)S(1)}, f32[48,32,128]{2,1,0:T(8,128)S(1)}, u32[]{:S(2)}, u32[]{:S(2)}) %collective-permute-start) | collective-permute-done | bytes 786464 | tf_op jit(solution)/shard_map/cond/branch_1_fun/ppermute | solution.py:697
  48.9 17.8 %collective-permute-done.1.refs_2_ = f32[48,32,128]{2,1,0:T(8,128)S(1)} collective-permute-done((f32[48,32,128]{2,1,0:T(8,128)S(1)}, f32[48,32,128]{2,1,0:T(8,128)S(1)}, u32[]{:S(2)}, u32[]{:S(2)}) %collective-permute-start.1) | collective-permute-done | bytes 786464 | tf_op jit(solution)/shard_map/cond/branch_1_fun/ppermute | solution.py:697
  66.8 1.4 deal_far.7
  69.4 1.7 all-to-all-done.near_ref
  71.1 9.9 %all-to-all-start.1 = ((f32[64,56,128]{2,1,0:T(8,128)}), f32[64,56,128]{2,1,0:T(8,128)}, u32[]{:S(2)}, u32[]{:S(2)}) async-start(f32[64,56,128]{2,1,0:T(8,128)} %copy-done.3), calls=%async_computation.1 | async-start | bytes 3670016 | tf_op jit(solution)/shard_map/cond/branch_1_fun/all_to_all | solution.py:701
  81.3 45.0 %all-to-all-done.1.far_ref = f32[64,56,128]{2,1,0:T(8,128)} async-done(((f32[64,56,128]{2,1,0:T(8,128)}), f32[64,56,128]{2,1,0:T(8,128)}, u32[]{:S(2)}, u32[]{:S(2)}) %all-to-all-start.1) | async-done | bytes 1835040 | tf_op jit(solution)/shard_map/cond/branch_1_fun/all_to_all | solution.py:701
  126.3 12.3 %solve.5 = (f32[64,56,128]{2,1,0:T(8,128)S(1)}, f32[64,56,128]{2,1,0:T(8,128)S(1)}) custom-call(s32[1]{0:T(128)} %get-tuple-element.317.place_ref, s32[8,128]{1,0:T(8,128)S(1)} %get-tuple-element.315.pos_ref, s32[1536]{0:T(1024)S(1)} %reshape.84.anchor_ref, f32[64,56,128]{2,1,0:T(8,128)S(1)} %all-to-all-done.near_ref, f32[64,56,128]{2,1,0:T(8,128)} %all-to-all-done.1.far_ref), custom_call_target="tpu_custom_call" | custom-call | flops 100000000 | bytes 30000000 | tf_op jit(solution)/shard_map/cond/branch_1_fun/solve/pallas_call | solution.py:554
  138.7 51.3 %all_to_all.42.terms_ref.table_ref = f32[64,56,128]{2,1,0:T(8,128)S(1)} all-to-all(f32[64,56,128]{2,1,0:T(8,128)S(1)} %get-tuple-element.323), channel_id=1, replica_groups=mesh['grp'=4,'grid'=64] {'grid'}, dimensions={0} | all-to-all | bytes 3670016 | tf_op jit(solution)/shard_map/cond/branch_1_fun/all_to_all | solution.py:701
  189.9 6.2 %all-to-all-start.3 = ((f32[64,56,128]{2,1,0:T(8,128)}), f32[64,56,128]{2,1,0:T(8,128)}, u32[]{:S(2)}, u32[]{:S(2)}) async-start(f32[64,56,128]{2,1,0:T(8,128)} %copy-done.4), calls=%async_computation.3 | async-start | bytes 3670016 | tf_op jit(solution)/shard_map/cond/branch_1_fun/all_to_all | solution.py:701
  196.2 1.8 back.3
  198.0 2.1 collective-permute-start.3
  201.4 2.6 %add_far.3.sum_ref = f32[130,32,128]{2,1,0:T(8,128)S(1)} custom-call(s32[8,128]{1,0:T(8,128)S(1)} %get-tuple-element.315.pos_ref, f32[64,56,128]{2,1,0:T(8,128)S(1)} %all_to_all.42.terms_ref.table_ref), custom_call_target="tpu_custom_call" | custom-call | flops 2000000 | bytes 4000000 | tf_op jit(solution)/shard_map/cond/branch_1_fun/add_far/pallas_call | solution.py:595
  204.0 12.9 %collective-permute-done.3.refs_0_ = f32[48,32,128]{2,1,0:T(8,128)S(1)} collective-permute-done((f32[48,32,128]{2,1,0:T(8,128)S(1)}, f32[48,32,128]{2,1,0:T(8,128)S(1)}, u32[]{:S(2)}, u32[]{:S(2)}) %collective-permute-start.3) | collective-permute-done | bytes 786464 | tf_op jit(solution)/shard_map/cond/branch_1_fun/ppermute | solution.py:697
  216.9 3.2 %collective-permute-done.4.refs_1_ = f32[48,32,128]{2,1,0:T(8,128)S(1)} collective-permute-done((f32[48,32,128]{2,1,0:T(8,128)S(1)}, f32[48,32,128]{2,1,0:T(8,128)S(1)}, u32[]{:S(2)}, u32[]{:S(2)}) %collective-permute-start.4) | collective-permute-done | bytes 786464 | tf_op jit(solution)/shard_map/cond/branch_1_fun/ppermute | solution.py:697
  220.1 18.0 %collective-permute-done.5.refs_2_ = f32[48,32,128]{2,1,0:T(8,128)S(1)} collective-permute-done((f32[48,32,128]{2,1,0:T(8,128)S(1)}, f32[48,32,128]{2,1,0:T(8,128)S(1)}, u32[]{:S(2)}, u32[]{:S(2)}) %collective-permute-start.5) | collective-permute-done | bytes 786464 | tf_op jit(solution)/shard_map/cond/branch_1_fun/ppermute | solution.py:697
  238.1 1.8 add_arrived.3.sum_ref
  239.9 1.4 copy-done.1
  241.5 4.9 %add_near.3 = f32[128,4096]{1,0:T(8,128)} custom-call(s32[8,128]{1,0:T(8,128)S(1)} %get-tuple-element.315.pos_ref, f32[130,32,128]{2,1,0:T(8,128)} %copy-done.1, f32[64,56,128]{2,1,0:T(8,128)} %all-to-all-done.3.terms_ref), custom_call_target="tpu_custom_call" | custom-call | flops 2000000 | bytes 10000000 | tf_op jit(solution)/shard_map/cond/branch_1_fun/add_near/pallas_call | solution.py:676
  (17 shorter events, 7.6 us)
Async XLA Ops:
  12.5 58.6 %all-to-all-start = ((f32[64,56,128]{2,1,0:T(8,128)}), f32[64,56,128]{2,1,0:T(8,128)S(1)}, u32[]{:S(2)}, u32[]{:S(2)}) async-start(f32[64,56,128]{2,1,0:T(8,128)} %deal_near.3), calls=%async_computation | async-start | bytes 3670016 | tf_op jit(solution)/shard_map/cond/branch_1_fun/all_to_all | solution.py:701
  29.0 19.9 %collective-permute-start = (f32[48,32,128]{2,1,0:T(8,128)S(1)}, f32[48,32,128]{2,1,0:T(8,128)S(1)}, u32[]{:S(2)}, u32[]{:S(2)}) collective-permute-start(f32[48,32,128]{2,1,0:T(8,128)S(1)} %get-tuple-element.320), channel_id=1, source_target_pairs={{0,64},{64,128},{128,192},{192,0},{1,65},{65,129},{129,193},{193,1... | collective-permute-start | bytes 2359304 | tf_op jit(solution)/shard_map/cond/branch_1_fun/ppermute | solution.py:697
  30.3 36.5 %collective-permute-start.1 = (f32[48,32,128]{2,1,0:T(8,128)S(1)}, f32[48,32,128]{2,1,0:T(8,128)S(1)}, u32[]{:S(2)}, u32[]{:S(2)}) collective-permute-start(f32[48,32,128]{2,1,0:T(8,128)S(1)} %get-tuple-element.321), channel_id=1, source_target_pairs={{0,128},{64,192},{128,0},{192,64},{1,129},{65,193},{129,1},{193,65... | collective-permute-start | bytes 2359304 | tf_op jit(solution)/shard_map/cond/branch_1_fun/ppermute | solution.py:697
  32.7 34.1 %collective-permute-start.2 = (f32[48,32,128]{2,1,0:T(8,128)S(1)}, f32[48,32,128]{2,1,0:T(8,128)S(1)}, u32[]{:S(2)}, u32[]{:S(2)}) collective-permute-start(f32[48,32,128]{2,1,0:T(8,128)S(1)} %get-tuple-element.322), channel_id=1, source_target_pairs={{0,192},{64,0},{128,64},{192,128},{1,193},{65,1},{129,65},{193,129... | collective-permute-start | bytes 2359304 | tf_op jit(solution)/shard_map/cond/branch_1_fun/ppermute | solution.py:697
  68.2 1.2 copy-start.3
  69.4 11.6 %copy-start.9 = (s32[512,3]{0,1:T(4,128)S(1)}, s32[512,3]{0,1:T(4,128)}, u32[]{:S(2)}) copy-start(s32[512,3]{0,1:T(4,128)} %get-tuple-element.368) | copy-start | bytes 18436 | tf_op jit(solution)/shard_map/cond
  71.1 55.2 %all-to-all-start.1 = ((f32[64,56,128]{2,1,0:T(8,128)}), f32[64,56,128]{2,1,0:T(8,128)}, u32[]{:S(2)}, u32[]{:S(2)}) async-start(f32[64,56,128]{2,1,0:T(8,128)} %copy-done.3), calls=%async_computation.1 | async-start | bytes 3670016 | tf_op jit(solution)/shard_map/cond/branch_1_fun/all_to_all | solution.py:701
  138.6 51.3 %copy-start.4 = (f32[64,56,128]{2,1,0:T(8,128)}, f32[64,56,128]{2,1,0:T(8,128)S(1)}, u32[]{:S(2)}) copy-start(f32[64,56,128]{2,1,0:T(8,128)S(1)} %get-tuple-element.328) | copy-start | bytes 5505028 | tf_op jit(solution)/shard_map/cond
  189.9 51.6 %all-to-all-start.3 = ((f32[64,56,128]{2,1,0:T(8,128)}), f32[64,56,128]{2,1,0:T(8,128)}, u32[]{:S(2)}, u32[]{:S(2)}) async-start(f32[64,56,128]{2,1,0:T(8,128)} %copy-done.4), calls=%async_computation.3 | async-start | bytes 3670016 | tf_op jit(solution)/shard_map/cond/branch_1_fun/all_to_all | solution.py:701
  198.0 18.9 %collective-permute-start.3 = (f32[48,32,128]{2,1,0:T(8,128)S(1)}, f32[48,32,128]{2,1,0:T(8,128)S(1)}, u32[]{:S(2)}, u32[]{:S(2)}) collective-permute-start(f32[48,32,128]{2,1,0:T(8,128)S(1)} %get-tuple-element.325), channel_id=1, source_target_pairs={{0,192},{64,0},{128,64},{192,128},{1,193},{65,1},{129,65},{193,129... | collective-permute-start | bytes 2359304 | tf_op jit(solution)/shard_map/cond/branch_1_fun/ppermute | solution.py:697
  200.2 19.9 %collective-permute-start.4 = (f32[48,32,128]{2,1,0:T(8,128)S(1)}, f32[48,32,128]{2,1,0:T(8,128)S(1)}, u32[]{:S(2)}, u32[]{:S(2)}) collective-permute-start(f32[48,32,128]{2,1,0:T(8,128)S(1)} %get-tuple-element.326), channel_id=1, source_target_pairs={{0,128},{64,192},{128,0},{192,64},{1,129},{65,193},{129,1},{193,65... | collective-permute-start | bytes 2359304 | tf_op jit(solution)/shard_map/cond/branch_1_fun/ppermute | solution.py:697
  201.0 37.1 %collective-permute-start.5 = (f32[48,32,128]{2,1,0:T(8,128)S(1)}, f32[48,32,128]{2,1,0:T(8,128)S(1)}, u32[]{:S(2)}, u32[]{:S(2)}) collective-permute-start(f32[48,32,128]{2,1,0:T(8,128)S(1)} %get-tuple-element.327), channel_id=1, source_target_pairs={{0,64},{64,128},{128,192},{192,0},{1,65},{65,129},{129,193},{193,1... | collective-permute-start | bytes 2359304 | tf_op jit(solution)/shard_map/cond/branch_1_fun/ppermute | solution.py:697
  239.9 1.4 copy-start.1

commit v3 on v2

--- a/solution.py
+++ b/solution.py
@@ -295,7 +295,7 @@
             table[pl.ds(i * 8 + 1, 8), k * 8 : k * 8 + 8] = jnp.swapaxes(jnp.stack(lines), 0, 1)
             return carry
 
-        lax.fori_loop(0, 128 // 8, lay_out, 0, unroll=2)
+        lax.fori_loop(0, 128 // 8, lay_out, 0, unroll=4)
     pushes = []
     for k in range(PARTS):
 
@@ -652,7 +652,7 @@
                 add_lines(flat(acc), pos_ref[0, q], its_lines(s, pos_ref[5, q], lines))
             return carry
 
-        lax.fori_loop(k * (B // PARTS), (k + 1) * (B // PARTS), here, 0, unroll=2)
+        lax.fori_loop(k * (B // PARTS), (k + 1) * (B // PARTS), here, 0, unroll=8)
     pushes = []
     for k in range(PARTS):
 
@@ -663,7 +663,7 @@
                 stage[k, rows, j * 128 : (j + 1) * 128] = lines[j]
             return carry
 
-        lax.fori_loop(0, 128 // 8, lay_out, 0, unroll=2)
+        lax.fori_loop(0, 128 // 8, lay_out, 0, unroll=4)
         pushes.append(pltpu.make_async_copy(stage.at[k], out_ref.at[:, pl.ds(k * 1024, 1024)], sem_out.at[k]))
         pushes[-1].start()
     for copy in pushes:

time: 247 us -> 247 us (level)
  no operation moved by 1% of the time
where the time goes in v3:
time: 247 us
  waiting for transfers between devices  114 us (46%)
  blocking collectives  51.2 us (21%)
  starting transfers between devices  37.4 us (15%)
  Pallas kernels  37 us (15%)
  local copies, waits for them, and re-layouts  5.59 us (2%)
    ppermute x6, waiting for transfers between devices, turned(): lax.ppermute(x, 'grp', [(g, (g + shift) % groups) for g in range(groups)])  67 us
    all_to_all x1, blocking collectives, exchanged(): return lax.all_to_all(planes, 'grid', 0, 0, tiled=True)  51.2 us
    all_to_all x3, waiting for transfers between devices, exchanged(): return lax.all_to_all(planes, 'grid', 0, 0, tiled=True)  47 us
    all_to_all x3, starting transfers between devices, exchanged(): return lax.all_to_all(planes, 'grid', 0, 0, tiled=True)  29.3 us
    pallas_call x1, Pallas kernels, solve(): pl.pallas_call(pair_kernel, out_shape=[jax.ShapeDtypeStruct(near.shape, j...  12.4 us
    ppermute x6, starting transfers between devices, turned(): lax.ppermute(x, 'grp', [(g, (g + shift) % groups) for g in range(groups)])  8.14 us
    pallas_call x1, Pallas kernels, route(): pl.pallas_call(route_kernel, out_shape=[jax.ShapeDtypeStruct((8, 128), jn...  7.35 us
  transfers between devices with their start and end apart: 9, of which 8 were waited for; matrix products, arithmetic and copies ran while one was open for 1% of the time, Pallas kernels for 3%

profile of v3, /device:TPU:1, one launch (start us, length us, event | category | flops | bytes accessed | tf_op | source)
XLA Modules:
  0.0 246.5 jit_solution(975273666179469048)
XLA Ops:
  0.7 7.4 %route.1 = (s32[8,128]{1,0:T(8,128)S(1)}, s32[8,256]{1,0:T(8,128)S(1)}, s32[8,256]{1,0:T(8,128)S(1)}, s32[1]{0:T(128)}) custom-call(s32[1]{0:T(128)} %bitcast.3.me_ref, s32[8,256]{1,0:T(8,128)S(1)} %reshape.87.pair_ref, s32[3,512]{1,0:T(4,128)} %bitcast.34), custom_call_target="tpu_custom_call" | custom-call | flops 10000000 | bytes 1000000 | tf_op jit(solution)/shard_map/route/pallas_call | solution.py:201
  8.7 237.6 %conditional.4 = (f32[128,4096]{1,0:T(8,128)}) conditional(s32[]{:T(128)} %bitcast.6, (s32[1]{0:T(128)}, s32[256,4,2]{0,2,1:T(2,128)}, f32[128,4096]{1,0:T(8,128)}, s32[512,3]{0,1:T(4,128)}, s32[1]{0:T(128)}, /*index=5*/s32[8,128]{1,0:T(8,128)S(1)}, s32[8,256]{1,0:T(8,128)S(1)}, s32[8,256]{1,0:T(8,128)S(1)}) %tuple.65, (s32[512,3]{0,1:T(4,128)}, ...), branch_computations={%region_0.12_spmd, %region_12.13_spmd} | conditional | flops 111966608 | bytes 313824512 | solution.py:799
  8.9 3.6 %deal_near.3 = f32[64,56,128]{2,1,0:T(8,128)} custom-call(s32[8,128]{1,0:T(8,128)S(1)} %get-tuple-element.315.pos_ref, f32[128,4096]{1,0:T(8,128)} %get-tuple-element.319.orb_ref), custom_call_target="tpu_custom_call" | custom-call | flops 2000000 | bytes 10000000 | tf_op jit(solution)/shard_map/cond/branch_1_fun/deal_near/pallas_call | solution.py:317
  12.5 13.2 %all-to-all-start = ((f32[64,56,128]{2,1,0:T(8,128)}), f32[64,56,128]{2,1,0:T(8,128)S(1)}, u32[]{:S(2)}, u32[]{:S(2)}) async-start(f32[64,56,128]{2,1,0:T(8,128)} %deal_near.3), calls=%async_computation | async-start | bytes 3670016 | tf_op jit(solution)/shard_map/cond/branch_1_fun/all_to_all | solution.py:701
  25.7 2.0 copy.20
  30.3 2.4 collective-permute-start.1
  33.9 15.1 %collective-permute-done.refs_1_ = f32[48,32,128]{2,1,0:T(8,128)S(1)} collective-permute-done((f32[48,32,128]{2,1,0:T(8,128)S(1)}, f32[48,32,128]{2,1,0:T(8,128)S(1)}, u32[]{:S(2)}, u32[]{:S(2)}) %collective-permute-start) | collective-permute-done | bytes 786464 | tf_op jit(solution)/shard_map/cond/branch_1_fun/ppermute | solution.py:697
  48.9 17.8 %collective-permute-done.1.refs_2_ = f32[48,32,128]{2,1,0:T(8,128)S(1)} collective-permute-done((f32[48,32,128]{2,1,0:T(8,128)S(1)}, f32[48,32,128]{2,1,0:T(8,128)S(1)}, u32[]{:S(2)}, u32[]{:S(2)}) %collective-permute-start.1) | collective-permute-done | bytes 786464 | tf_op jit(solution)/shard_map/cond/branch_1_fun/ppermute | solution.py:697
  66.8 1.4 deal_far.7
  69.4 1.7 all-to-all-done.near_ref
  71.1 9.9 %all-to-all-start.1 = ((f32[64,56,128]{2,1,0:T(8,128)}), f32[64,56,128]{2,1,0:T(8,128)}, u32[]{:S(2)}, u32[]{:S(2)}) async-start(f32[64,56,128]{2,1,0:T(8,128)} %copy-done.3), calls=%async_computation.1 | async-start | bytes 3670016 | tf_op jit(solution)/shard_map/cond/branch_1_fun/all_to_all | solution.py:701
  81.3 45.0 %all-to-all-done.1.far_ref = f32[64,56,128]{2,1,0:T(8,128)} async-done(((f32[64,56,128]{2,1,0:T(8,128)}), f32[64,56,128]{2,1,0:T(8,128)}, u32[]{:S(2)}, u32[]{:S(2)}) %all-to-all-start.1) | async-done | bytes 1835040 | tf_op jit(solution)/shard_map/cond/branch_1_fun/all_to_all | solution.py:701
  126.3 12.4 %solve.5 = (f32[64,56,128]{2,1,0:T(8,128)S(1)}, f32[64,56,128]{2,1,0:T(8,128)S(1)}) custom-call(s32[1]{0:T(128)} %get-tuple-element.317.place_ref, s32[8,128]{1,0:T(8,128)S(1)} %get-tuple-element.315.pos_ref, s32[1536]{0:T(1024)S(1)} %reshape.84.anchor_ref, f32[64,56,128]{2,1,0:T(8,128)S(1)} %all-to-all-done.near_ref, f32[64,56,128]{2,1,0:T(8,128)} %all-to-all-done.1.far_ref), custom_call_target="tpu_custom_call" | custom-call | flops 100000000 | bytes 30000000 | tf_op jit(solution)/shard_map/cond/branch_1_fun/solve/pallas_call | solution.py:554
  138.7 51.2 %all_to_all.42.terms_ref.table_ref = f32[64,56,128]{2,1,0:T(8,128)S(1)} all-to-all(f32[64,56,128]{2,1,0:T(8,128)S(1)} %get-tuple-element.323), channel_id=1, replica_groups=mesh['grp'=4,'grid'=64] {'grid'}, dimensions={0} | all-to-all | bytes 3670016 | tf_op jit(solution)/shard_map/cond/branch_1_fun/all_to_all | solution.py:701
  190.0 6.2 %all-to-all-start.3 = ((f32[64,56,128]{2,1,0:T(8,128)}), f32[64,56,128]{2,1,0:T(8,128)}, u32[]{:S(2)}, u32[]{:S(2)}) async-start(f32[64,56,128]{2,1,0:T(8,128)} %copy-done.4), calls=%async_computation.3 | async-start | bytes 3670016 | tf_op jit(solution)/shard_map/cond/branch_1_fun/all_to_all | solution.py:701
  196.2 1.8 back.3
  198.1 2.1 collective-permute-start.3
  201.3 2.6 %add_far.3.sum_ref = f32[130,32,128]{2,1,0:T(8,128)S(1)} custom-call(s32[8,128]{1,0:T(8,128)S(1)} %get-tuple-element.315.pos_ref, f32[64,56,128]{2,1,0:T(8,128)S(1)} %all_to_all.42.terms_ref.table_ref), custom_call_target="tpu_custom_call" | custom-call | flops 2000000 | bytes 4000000 | tf_op jit(solution)/shard_map/cond/branch_1_fun/add_far/pallas_call | solution.py:595
  204.0 12.9 %collective-permute-done.3.refs_0_ = f32[48,32,128]{2,1,0:T(8,128)S(1)} collective-permute-done((f32[48,32,128]{2,1,0:T(8,128)S(1)}, f32[48,32,128]{2,1,0:T(8,128)S(1)}, u32[]{:S(2)}, u32[]{:S(2)}) %collective-permute-start.3) | collective-permute-done | bytes 786464 | tf_op jit(solution)/shard_map/cond/branch_1_fun/ppermute | solution.py:697
  216.9 3.2 %collective-permute-done.4.refs_1_ = f32[48,32,128]{2,1,0:T(8,128)S(1)} collective-permute-done((f32[48,32,128]{2,1,0:T(8,128)S(1)}, f32[48,32,128]{2,1,0:T(8,128)S(1)}, u32[]{:S(2)}, u32[]{:S(2)}) %collective-permute-start.4) | collective-permute-done | bytes 786464 | tf_op jit(solution)/shard_map/cond/branch_1_fun/ppermute | solution.py:697
  220.1 18.0 %collective-permute-done.5.refs_2_ = f32[48,32,128]{2,1,0:T(8,128)S(1)} collective-permute-done((f32[48,32,128]{2,1,0:T(8,128)S(1)}, f32[48,32,128]{2,1,0:T(8,128)S(1)}, u32[]{:S(2)}, u32[]{:S(2)}) %collective-permute-start.5) | collective-permute-done | bytes 786464 | tf_op jit(solution)/shard_map/cond/branch_1_fun/ppermute | solution.py:697
  238.1 1.8 add_arrived.3.sum_ref
  239.9 1.4 copy-done.1
  241.6 4.7 %add_near.3 = f32[128,4096]{1,0:T(8,128)} custom-call(s32[8,128]{1,0:T(8,128)S(1)} %get-tuple-element.315.pos_ref, f32[130,32,128]{2,1,0:T(8,128)} %copy-done.1, f32[64,56,128]{2,1,0:T(8,128)} %all-to-all-done.3.terms_ref), custom_call_target="tpu_custom_call" | custom-call | flops 2000000 | bytes 10000000 | tf_op jit(solution)/shard_map/cond/branch_1_fun/add_near/pallas_call | solution.py:676
  (17 shorter events, 7.6 us)
Async XLA Ops:
  12.5 58.6 %all-to-all-start = ((f32[64,56,128]{2,1,0:T(8,128)}), f32[64,56,128]{2,1,0:T(8,128)S(1)}, u32[]{:S(2)}, u32[]{:S(2)}) async-start(f32[64,56,128]{2,1,0:T(8,128)} %deal_near.3), calls=%async_computation | async-start | bytes 3670016 | tf_op jit(solution)/shard_map/cond/branch_1_fun/all_to_all | solution.py:701
  29.0 19.9 %collective-permute-start = (f32[48,32,128]{2,1,0:T(8,128)S(1)}, f32[48,32,128]{2,1,0:T(8,128)S(1)}, u32[]{:S(2)}, u32[]{:S(2)}) collective-permute-start(f32[48,32,128]{2,1,0:T(8,128)S(1)} %get-tuple-element.320), channel_id=1, source_target_pairs={{0,64},{64,128},{128,192},{192,0},{1,65},{65,129},{129,193},{193,1... | collective-permute-start | bytes 2359304 | tf_op jit(solution)/shard_map/cond/branch_1_fun/ppermute | solution.py:697
  30.3 36.5 %collective-permute-start.1 = (f32[48,32,128]{2,1,0:T(8,128)S(1)}, f32[48,32,128]{2,1,0:T(8,128)S(1)}, u32[]{:S(2)}, u32[]{:S(2)}) collective-permute-start(f32[48,32,128]{2,1,0:T(8,128)S(1)} %get-tuple-element.321), channel_id=1, source_target_pairs={{0,128},{64,192},{128,0},{192,64},{1,129},{65,193},{129,1},{193,65... | collective-permute-start | bytes 2359304 | tf_op jit(solution)/shard_map/cond/branch_1_fun/ppermute | solution.py:697
  32.7 34.1 %collective-permute-start.2 = (f32[48,32,128]{2,1,0:T(8,128)S(1)}, f32[48,32,128]{2,1,0:T(8,128)S(1)}, u32[]{:S(2)}, u32[]{:S(2)}) collective-permute-start(f32[48,32,128]{2,1,0:T(8,128)S(1)} %get-tuple-element.322), channel_id=1, source_target_pairs={{0,192},{64,0},{128,64},{192,128},{1,193},{65,1},{129,65},{193,129... | collective-permute-start | bytes 2359304 | tf_op jit(solution)/shard_map/cond/branch_1_fun/ppermute | solution.py:697
  68.1 1.2 copy-start.3
  69.4 11.6 %copy-start.9 = (s32[512,3]{0,1:T(4,128)S(1)}, s32[512,3]{0,1:T(4,128)}, u32[]{:S(2)}) copy-start(s32[512,3]{0,1:T(4,128)} %get-tuple-element.368) | copy-start | bytes 18436 | tf_op jit(solution)/shard_map/cond
  71.1 55.2 %all-to-all-start.1 = ((f32[64,56,128]{2,1,0:T(8,128)}), f32[64,56,128]{2,1,0:T(8,128)}, u32[]{:S(2)}, u32[]{:S(2)}) async-start(f32[64,56,128]{2,1,0:T(8,128)} %copy-done.3), calls=%async_computation.1 | async-start | bytes 3670016 | tf_op jit(solution)/shard_map/cond/branch_1_fun/all_to_all | solution.py:701
  138.7 51.3 %copy-start.4 = (f32[64,56,128]{2,1,0:T(8,128)}, f32[64,56,128]{2,1,0:T(8,128)S(1)}, u32[]{:S(2)}) copy-start(f32[64,56,128]{2,1,0:T(8,128)S(1)} %get-tuple-element.328) | copy-start | bytes 5505028 | tf_op jit(solution)/shard_map/cond
  190.0 51.6 %all-to-all-start.3 = ((f32[64,56,128]{2,1,0:T(8,128)}), f32[64,56,128]{2,1,0:T(8,128)}, u32[]{:S(2)}, u32[]{:S(2)}) async-start(f32[64,56,128]{2,1,0:T(8,128)} %copy-done.4), calls=%async_computation.3 | async-start | bytes 3670016 | tf_op jit(solution)/shard_map/cond/branch_1_fun/all_to_all | solution.py:701
  198.1 18.8 %collective-permute-start.3 = (f32[48,32,128]{2,1,0:T(8,128)S(1)}, f32[48,32,128]{2,1,0:T(8,128)S(1)}, u32[]{:S(2)}, u32[]{:S(2)}) collective-permute-start(f32[48,32,128]{2,1,0:T(8,128)S(1)} %get-tuple-element.325), channel_id=1, source_target_pairs={{0,192},{64,0},{128,64},{192,128},{1,193},{65,1},{129,65},{193,129... | collective-permute-start | bytes 2359304 | tf_op jit(solution)/shard_map/cond/branch_1_fun/ppermute | solution.py:697
  200.2 19.9 %collective-permute-start.4 = (f32[48,32,128]{2,1,0:T(8,128)S(1)}, f32[48,32,128]{2,1,0:T(8,128)S(1)}, u32[]{:S(2)}, u32[]{:S(2)}) collective-permute-start(f32[48,32,128]{2,1,0:T(8,128)S(1)} %get-tuple-element.326), channel_id=1, source_target_pairs={{0,128},{64,192},{128,0},{192,64},{1,129},{65,193},{129,1},{193,65... | collective-permute-start | bytes 2359304 | tf_op jit(solution)/shard_map/cond/branch_1_fun/ppermute | solution.py:697
  201.0 37.1 %collective-permute-start.5 = (f32[48,32,128]{2,1,0:T(8,128)S(1)}, f32[48,32,128]{2,1,0:T(8,128)S(1)}, u32[]{:S(2)}, u32[]{:S(2)}) collective-permute-start(f32[48,32,128]{2,1,0:T(8,128)S(1)} %get-tuple-element.327), channel_id=1, source_target_pairs={{0,64},{64,128},{128,192},{192,0},{1,65},{65,129},{129,193},{193,1... | collective-permute-start | bytes 2359304 | tf_op jit(solution)/shard_map/cond/branch_1_fun/ppermute | solution.py:697
  239.9 1.4 copy-start.1
